TPU v7x, 32 devices: a whole 2x2x4 slice. The times are simulated.
32 devices in a mesh: rep: 8 (over y, x, core), tp: 4 (over z).
Axes of the slice: x: 2, y: 2, z: 4, core: 2. Of those that a mesh axis runs over, the one named last changes fastest.
Arguments:
- tokens: bfloat16 [128, 1024], P('rep'), may hold values from -6 to 6
- lengths: int32 [128], P('rep'), may hold values from 1 to 256, as said below
- prompt_group: int32 [128], P('rep'), may hold values from 0 to 7
- span_close: int32 [128], P('rep'), may hold values 0 or 1
- out_slot: int32 [8, 2], P('rep'), may hold values from 0 to 15, as said below
- move_dest: int32 [8, 2], P('rep'), may hold values from 0 to 7, as said below
- page_table: int32 [128, 2, 1], P('rep'), may hold values from 0 to 15, as said below
- cache_pool: bfloat16 [128, 16, 128, 256], P('rep', 'tp'), may hold values from -6 to 6
- prefix_cache: bfloat16 [8, 16, 64, 256], P(None, 'tp'), may hold values from -6 to 6
- memory: float32 [128, 16, 64, 128], P('rep', 'tp'), may hold values from -2 to 2
- norm_attn: float32 [1024], replicated, may hold values from 0.5 to 1.5
- norm_mlp: float32 [1024], replicated, may hold values from 0.5 to 1.5
- qkv_weight: bfloat16 [1024, 3072], P(None, 'tp'), may hold values from -0.1875 to 0.1875
- out_weight: bfloat16 [1024, 1024], P('tp'), may hold values from -0.1875 to 0.1875
- gate_weight: bfloat16 [1024, 2816], P(None, 'tp'), may hold values from -0.1875 to 0.1875
- up_weight: bfloat16 [1024, 2816], P(None, 'tp'), may hold values from -0.1875 to 0.1875
- down_weight: bfloat16 [2816, 1024], P('tp'), may hold values from -0.109375 to 0.109375
- forget: float32 [8], replicated, may hold values from 0.5 to 0.99
- write_rate: float32 [8], replicated, may hold values from 0.1 to 0.9
Outputs:
- out_rows: bfloat16 [128, 1024], P('rep')
- new_memory: float32 [128, 16, 64, 128], P('rep', 'tp')
- new_cache_pool: bfloat16 [128, 16, 128, 256], P('rep', 'tp')
Inputs may be any that keep to these rules, and one draw needn't show every extreme that they name: `lengths`: the cached tokens of a request; some request of every replica holds 256. `out_slot`: the 2 slots of one replica are distinct. For each m, move_dest[:, m] is a permutation of the replicas. `page_table`: for each replica and half, the entries of its 16 slots are a permutation of 0 to 15.
All inputs are finite; a program needn't handle non-finite values. No bound on the sum of `span_close` on one device may be relied on, other than what follows from the above.
Results may differ from a plain program's by a relative error of at most 0.013.
Values may be sent and summed in bfloat16 or wider, within the bound.
A program may use at most 64 MiB of HBM per device.

v0:
```python
import jax
import jax.numpy as jnp
from jax import lax
from jax.sharding import PartitionSpec as P

highest = lax.Precision.HIGHEST


def from_partner(block, axis, apart):
    count = lax.axis_size(axis)
    route = []
    for low in range(count):
        high = low | 1 << apart
        if high != low and high < count:
            route += [(low, high), (high, low)]
    return lax.ppermute(block, axis, route)


def rms_scale(values, gain_vec):
    return values * lax.rsqrt(jnp.mean(values * values, axis=-1, keepdims=True) + 1e-05) * gain_vec


def unit_rows(values):
    return values * lax.rsqrt(jnp.sum(values * values, axis=-1, keepdims=True) + 1e-06)


def join_pair(part_one, part_two):
    top_one, denom_one, accum_one = part_one
    top_two, denom_two, accum_two = part_two
    top_score = jnp.maximum(top_one, top_two)
    weight_one = jnp.exp(top_one - top_score)
    weight_two = jnp.exp(top_two - top_score)
    return (
        top_score,
        denom_one * weight_one + denom_two * weight_two,
        accum_one * weight_one[..., None] + accum_two * weight_two[..., None],
    )


def picked_rows(dest_rows, my_rep, move_count):
    row_count = dest_rows.shape[0]
    row_move = jnp.arange(row_count) % move_count
    return (dest_rows == my_rep)[:, None] & (row_move[:, None] == jnp.arange(move_count)[None, :])


def body(
    tokens,
    lengths,
    prompt_group,
    span_close,
    out_slot,
    move_dest,
    page_table,
    cache_pool,
    prefix_cache,
    memory,
    norm_attn,
    norm_mlp,
    qkv_weight,
    out_weight,
    gate_weight,
    up_weight,
    down_weight,
    forget,
    write_rate,
):
    req_count = tokens.shape[0]
    model_dim = tokens.shape[1]
    sect_count = cache_pool.shape[1]
    page_len = cache_pool.shape[2]
    half_dim = memory.shape[2]
    head_dim = memory.shape[3]
    head_count = forget.shape[0]
    group_count = prefix_cache.shape[0]
    move_count = out_slot.shape[1]
    page_count = page_table.shape[2]
    sections = lax.axis_index("tp") * sect_count + jnp.arange(sect_count)
    halves = sections // head_count
    head_ids = sections % head_count
    sect_index = jnp.arange(sect_count)[None, :, None]
    moved_slots = out_slot[0]
    page_ids = page_table[:, halves, :]
    slot_pages = page_ids[moved_slots]
    my_rep = lax.axis_index("rep")
    send_pages = cache_pool[slot_pages, sect_index].reshape(move_count, -1)
    dest_rows = lax.all_gather(move_dest[0], "rep", axis=0, tiled=True)
    page_rows = lax.all_gather(send_pages, "rep", axis=0, tiled=True)
    picked = picked_rows(dest_rows, my_rep, move_count)
    pages_in = jnp.dot(picked.astype(jnp.bfloat16).T, page_rows, preferred_element_type=jnp.float32)
    new_pool = cache_pool.at[slot_pages, sect_index].set(
        pages_in.astype(jnp.bfloat16).reshape(
            move_count, sect_count, page_count, page_len, 2 * head_dim
        )
    )
    residual_in = tokens.astype(jnp.float32)
    normed = rms_scale(residual_in, norm_attn).astype(jnp.bfloat16)
    qkv_part = jnp.dot(normed, qkv_weight, preferred_element_type=jnp.float32).astype(jnp.bfloat16)
    qkv_full = lax.all_gather(qkv_part, "tp", axis=1, tiled=True)
    queries = qkv_full[:, :model_dim].reshape(req_count, head_count, head_dim)[:, head_ids]
    keys_new = qkv_full[:, model_dim : 2 * model_dim].reshape(req_count, head_count, head_dim)[
        :, head_ids
    ]
    values_new = qkv_full[:, 2 * model_dim :].reshape(req_count, head_count, head_dim)[:, head_ids]
    score_scale = head_dim ** (-0.5)
    cached = cache_pool[page_ids, sect_index].reshape(req_count, sect_count, -1, 2 * head_dim)
    group_hot = (prompt_group[:, None] == jnp.arange(group_count)[None, :]).astype(jnp.bfloat16)
    prefix = jnp.einsum(
        "rg,gsnd->rsnd", group_hot, prefix_cache, preferred_element_type=jnp.float32
    ).astype(jnp.bfloat16)
    key_data = jnp.concatenate([prefix, cached], axis=2)
    positions = (
        (2 * jnp.arange(page_count)[None, :, None] + halves[:, None, None]) * page_len
        + jnp.arange(page_len)[None, None, :]
    ).reshape(sect_count, -1)
    live_keys = jnp.concatenate(
        [
            jnp.ones((req_count, sect_count, prefix.shape[2]), bool),
            positions[None, :, :] < lengths[:, None, None],
        ],
        axis=2,
    )
    scores = (
        jnp.einsum(
            "rsd,rsnd->rsn", queries, key_data[..., :head_dim], preferred_element_type=jnp.float32
        )
        * score_scale
    )
    scores = jnp.where(live_keys, scores, -jnp.inf)
    query_full = queries.astype(jnp.float32)
    key_full = keys_new.astype(jnp.float32)
    value_full = values_new.astype(jnp.float32)
    own_score = jnp.sum(query_full * key_full, axis=-1) * score_scale
    own_score = jnp.where(halves[None, :] == 0, own_score, -jnp.inf)
    top_score = jnp.maximum(jnp.max(scores, axis=-1), own_score)
    weights = jnp.exp(scores - top_score[..., None])
    own_weight = jnp.exp(own_score - top_score)
    denom_sum = jnp.sum(weights, axis=-1) + own_weight
    accumulated = jnp.einsum(
        "rsn,rsnd->rsd", weights, key_data[..., head_dim:].astype(jnp.float32), precision=highest
    )
    accumulated = accumulated + own_weight[..., None] * value_full
    partial_value = (top_score, denom_sum, accumulated)
    pair_bit = lax.axis_size("tp").bit_length() - 2
    partial_value = join_pair(
        partial_value,
        from_partner((partial_value[0], partial_value[1], partial_value[2]), "tp", pair_bit),
    )
    attended = partial_value[2] / partial_value[1][..., None]
    first_half = halves[None, :, None] == 0
    attn_half = jnp.where(first_half, attended[..., :half_dim], attended[..., half_dim:])
    query_unit = unit_rows(query_full)
    key_unit = unit_rows(key_full)
    recalled = jnp.einsum("rsij,rsj->rsi", memory, query_unit, precision=highest)
    mixed_out = (attn_half + recalled).astype(jnp.bfloat16).reshape(req_count, -1)
    attn_term = jnp.dot(mixed_out, out_weight, preferred_element_type=jnp.float32)
    hidden_in = residual_in + lax.psum(attn_term, "tp")
    normed_mlp = rms_scale(hidden_in, norm_mlp).astype(jnp.bfloat16)
    gate_out = jnp.dot(normed_mlp, gate_weight, preferred_element_type=jnp.float32)
    up_out = jnp.dot(normed_mlp, up_weight, preferred_element_type=jnp.float32)
    activated = (jax.nn.silu(gate_out) * up_out).astype(jnp.bfloat16)
    rows_done = (
        hidden_in
        + lax.psum(
            jnp.dot(activated, down_weight, preferred_element_type=jnp.float32).astype(
                jnp.bfloat16
            ),
            "tp",
        ).astype(jnp.float32)
    ).astype(jnp.bfloat16)
    predicted = jnp.einsum("rsij,rsj->rsi", memory, key_unit, precision=highest)
    value_half = jnp.where(first_half, value_full[..., :half_dim], value_full[..., half_dim:])
    misfit = value_half - predicted
    keep_rate = forget[head_ids][None, :, None, None]
    step_rate = write_rate[head_ids][None, :, None, None]
    updated = keep_rate * memory + step_rate * misfit[..., None] * key_unit[:, :, None, :]
    mem_after = jnp.where(span_close[:, None, None, None] == 1, updated, memory)
    send_rows = rows_done[moved_slots].astype(jnp.float32)
    send_memory = mem_after[moved_slots].reshape(move_count, -1)
    dest_rows = lax.all_gather(move_dest[0], "rep", axis=0, tiled=True)
    out_part = lax.all_gather(send_rows.astype(jnp.bfloat16), "rep", axis=0, tiled=True).astype(
        jnp.float32
    )
    memory_rows = lax.all_gather(
        send_memory.astype(jnp.bfloat16), "rep", axis=0, tiled=True
    ).astype(jnp.float32)
    picked = picked_rows(dest_rows, my_rep, move_count)
    pick_full = picked.astype(jnp.float32).T
    rows_in = jnp.zeros(send_rows.shape, jnp.float32)
    memory_in = jnp.zeros(send_memory.shape, jnp.float32)
    rows_in = rows_in + jnp.dot(pick_full, out_part, precision=highest)
    memory_in = memory_in + jnp.dot(pick_full, memory_rows, precision=highest)
    rows_in, memory_in = (rows_in, memory_in)
    rows_done = rows_done.at[moved_slots].set(rows_in.astype(jnp.bfloat16))
    mem_after = mem_after.at[moved_slots].set(
        memory_in.reshape(move_count, sect_count, half_dim, head_dim)
    )
    return (rows_done, mem_after, new_pool)


def solution(mesh):
    placed = (
        P("rep", None),
        P("rep"),
        P("rep"),
        P("rep"),
        P("rep", None),
        P("rep", None),
        P("rep", None, None),
        P("rep", "tp", None, None),
        P(None, "tp", None, None),
        P("rep", "tp", None, None),
        P(),
        P(),
        P(None, "tp"),
        P("tp", None),
        P(None, "tp"),
        P(None, "tp"),
        P("tp", None),
        P(),
        P(),
    )
    return jax.shard_map(
        body,
        mesh=mesh,
        in_specs=placed,
        out_specs=(P("rep", None), P("rep", "tp", None, None), P("rep", "tp", None, None)),
        check_vma=False,
    )
```

profile of v0, /device:TPU:0, one launch (start us, length us, event | category | flops | bytes accessed | tf_op | source)
XLA Modules:
  0.0 152.0 jit_solution(4708491910738600830)
XLA Ops:
  8.1 4.8 %copy.118 = bf16[16,4,128,256]{3,2,1,0:T(8,128)(2,1)} copy(bf16[16,4,128,256]{3,2,1,0:T(8,128)(2,1)} %param.26) | data formatting | bytes 8388608
  13.0 0.1 fusion.7
  13.1 0.4 convolution_convert_fusion.3
  13.5 15.0 %all_gather.16 = bf16[16,3072]{1,0:T(8,128)(2,1)S(1)} all-gather(bf16[16,768]{1,0:T(8,128)(2,1)S(1)} %convolution_convert_fusion.3), channel_id=1, replica_groups=mesh['rep'=8,'tp'=4] {'tp'}, dimensions={1}, use_global_device_ids=true | all-gather | bytes 122880 | tf_op jit(solution)/shard_map/all_gather | solution.py:98
  28.6 0.6 gather_fusion.3
  29.1 0.6 gather_fusion
  29.7 0.6 gather_fusion.1
  30.3 0.1 copy.64
  30.4 0.1 reshape.428
  30.5 0.8 convolution_convert_fusion.1
  31.4 2.0 %copy.65 = bf16[16,4,64,256]{3,2,1,0:T(8,128)(2,1)} copy(bf16[16,4,64,256]{3,0,2,1:T(8,128)(2,1)S(1)} %convolution_convert_fusion.1) | data formatting | bytes 4194304 | tf_op jit(solution)/shard_map/convert_element_type | solution.py:109
  33.5 0.1 fusion.27
  33.6 4.9 %gather_fusion.2 = bf16[64,128,256]{2,1,0:T(8,128)(2,1)} fusion(bf16[16,4,128,256]{3,2,1,0:T(8,128)(2,1)} %copy.118, s32[64]{0:T(128)S(1)} %reshape.428), kind=kCustom, calls=%fused_computation.2 | custom fusion | bytes 8389120 | tf_op jit(solution)/shard_map/gather | solution.py:105
  38.6 3.6 %fusion.3 = f32[16,4,1,192]{3,2,1,0:T(1,128)S(1)} fusion(bf16[16,4,64,256]{3,2,1,0:T(8,128)(2,1)} %copy.65, bf16[16,4,128,256]{3,2,1,0:T(8,128)(2,1)} %bitcast.105, bf16[16,4,128,1]{2,0,1,3:T(8,128)(2,1)S(1)} %bitcast.109), kind=kOutput, calls=%fused_computation.21 | convolution fusion | flops 9437184 | bytes 6356992 | tf_op jit(solution)/shard_map/rsd,rsnd->rsn/dot_general | solution.py:123
  42.2 0.2 fusion.35
  42.4 0.1 fusion.56
  42.5 0.6 collective-permute-start
  43.1 0.2 fusion.12
  43.3 0.6 gather_fusion.4
  43.9 4.5 %fusion.1 = f32[16,4,1,128]{3,2,1,0:T(1,128)S(1)} fusion(bf16[16,4,128,256]{3,2,1,0:T(8,128)(2,1)} %bitcast.106, bf16[16,4,64,256]{3,2,1,0:T(8,128)(2,1)} %copy.65, f32[16,4,192,1]{2,0,1,3:T(8,128)S(1)} %get-tuple-element.17), kind=kOutput, calls=%fused_computation.19 | convolution fusion | flops 25165824 | bytes 6373376 | tf_op jit(solution)/shard_map/rsn,rsnd->rsd/dot_general | solution.py:138
  48.4 0.1 fusion.68
  48.5 0.1 bitcast_add_fusion
  48.6 2.3 %collective-permute-start.1 = (f32[16,4,128]{2,0,1:T(8,128)S(1)}, f32[16,4,128]{2,0,1:T(8,128)S(1)}, u32[]{:S(2)}, u32[]{:S(2)}) collective-permute-start(f32[16,4,128]{2,0,1:T(8,128)S(1)} %bitcast_add_fusion), channel_id=1, source_target_pairs={{0,2},{2,0},{1,3},{3,1},{4,6},{6,4},{5,7},{7,5},{8,10},{10,8},{9,1... | collective-permute-start | bytes 98312 | tf_op jit(solution)/shard_map/ppermute | solution.py:16
  50.9 0.6 collective-permute-start.2
  51.7 3.4 %fusion.28 = f32[16,4,1,64]{3,2,1,0:T(1,128)S(1)} fusion(f32[16,4,64,128]{3,2,1,0:T(8,128)S(1)} %copy-done.3, f32[16,4,128,1]{2,0,1,3:T(8,128)S(1)} %get-tuple-element.18), kind=kOutput, calls=%fused_computation.73 | convolution fusion | flops 6291456 | bytes 2146304 | tf_op jit(solution)/shard_map/rsij,rsj->rsi/dot_general | solution.py:170
  55.1 3.4 %fusion.30 = f32[16,4,1,64]{3,2,1,0:T(1,128)S(1)} fusion(f32[16,4,64,128]{3,2,1,0:T(8,128)S(1)} %copy-done.3, f32[16,4,128,1]{2,0,1,3:T(8,128)S(1)} %fusion.21), kind=kOutput, calls=%fused_computation.75 | convolution fusion | flops 6291456 | bytes 2146304 | tf_op jit(solution)/shard_map/rsij,rsj->rsi/dot_general | solution.py:153
  58.5 0.6 gather_fusion.7
  59.2 0.6 gather_fusion.6
  59.9 0.1 add_divide_fusion
  60.0 0.1 fusion.24
  60.1 0.1 reshape.404
  60.2 0.8 fusion.69
  61.1 3.0 %add_select_fusion = f32[16,4,64,128]{3,2,1,0:T(8,128)} fusion(f32[16,4,64,128]{3,2,1,0:T(8,128)} %param.28, f32[16,4,128]{2,1,0:T(4,128)S(1)} %copy.70, f32[16,4,64]{2,1,0:T(4,128)S(1)} %copy.69, f32[4]{0:T(128)S(1)} %gather_fusion.6, pred[16]{0:T(512)(128)(4,1)S(1)} %broadcast_compare_fusion.2), kind=kLoop, calls=%fused_computation.22 | loop fusion | flops 2097152 | bytes 4243488 | tf_op jit(solution)/shard_map/jit(_where)/select_n | solution.py:176
  64.1 2.3 %gather_fusion.8 = bf16[2,4,64,128]{3,2,1,0:T(8,128)(2,1)S(1)} fusion(f32[16,4,64,128]{3,2,1,0:T(8,128)} %add_select_fusion, s32[1024]{0:T(1024)S(1)} %pad_clamp_fusion), kind=kCustom, calls=%fused_computation.8 | custom fusion | bytes 262152 | tf_op jit(solution)/shard_map/gather | solution.py:178
  66.3 0.7 reshape.542
  67.1 0.2 all-gather.10.cloned.1.call-start
  67.3 0.1 copy.71
  67.4 0.6 gather_fusion.9
  68.0 0.6 broadcast.575
  68.6 1.3 fusion.65
  69.8 0.1 reshape.494
  69.9 2.8 %gather_fusion.10 = bf16[8,128,256]{2,1,0:T(8,128)(2,1)S(1)} fusion(bf16[16,4,128,256]{3,2,1,0:T(8,128)(2,1)} %copy.118, s32[8]{0:T(128)S(1)} %reshape.494), kind=kCustom, calls=%fused_computation.10 | custom fusion | bytes 1048640 | tf_op jit(solution)/shard_map/gather | solution.py:85
  72.7 1.0 reshape.544
  73.7 1.2 dynamic-slice
  75.5 0.8 bitcast_dynamic-update-slice_fusion
  76.3 8.0 %all-reduce.1 = s32[16]{0:T(128)S(1)} all-reduce(s32[16]{0:T(128)S(1)} %bitcast_dynamic-update-slice_fusion), channel_id=2, replica_groups=mesh['rep'=8,'tp'=4] {'rep'}, use_global_device_ids=true, to_apply=%add.1 | all-reduce | flops 16 | bytes 128
  84.3 0.8 reshape.518
  85.0 11.2 %all-reduce.4.cloned.1.call-done = f32[16,1024]{1,0:T(8,128)} async-done(((f32[16,1024]{1,0:T(8,128)}), f32[16,1024]{1,0:T(8,128)}) %all-reduce.4.cloned.1.call-update) | async-done | bytes 65552 | tf_op jit(solution)/shard_map/psum | solution.py:156
  96.2 1.0 multiply_reduce_fusion
  97.2 0.9 multiply_convert_fusion
  98.1 0.5 fusion.70
  98.6 2.8 %convolution_convert_fusion.2 = bf16[16,1024]{1,0:T(8,128)(2,1)S(1)} fusion(bf16[704,1024]{1,0:T(8,128)(2,1)} %param.35, bf16[16,1024]{1,0:T(8,128)(2,1)S(1)} %multiply_convert_fusion, bf16[1024,704]{0,1:T(8,128)(2,1)} %param.34, f32[16,704]{1,0:T(8,128)S(1)} %fusion.70), kind=kOutput, calls=%fused_computation.25 | convolution fusion | flops 46221312 | bytes 2994176 | tf_op jit(solution)/shard_map/dot_general | solution.py:164
  101.5 17.6 %psum.15 = bf16[16,1024]{1,0:T(8,128)(2,1)S(1)} all-reduce(bf16[16,1024]{1,0:T(8,128)(2,1)S(1)} %convolution_convert_fusion.2), channel_id=1, replica_groups=mesh['rep'=8,'tp'=4] {'tp'}, use_global_device_ids=true, to_apply=%region_7.8 | all-reduce | flops 16384 | bytes 65536 | tf_op jit(solution)/shard_map/psum | solution.py:163
  119.2 0.6 gather_fusion.5
  119.7 9.2 %all-gather.2 = bf16[8,2,1024]{2,1,0:T(2,128)(2,1)S(1)} all-gather(bf16[1,2,1024]{2,1,0:T(2,128)(2,1)S(1)} %bitcast.112), channel_id=3, replica_groups=mesh['rep'=8,'tp'=4] {'rep'}, dimensions={0}, use_global_device_ids=true | all-gather | bytes 36864 | tf_op jit(solution)/shard_map/all_gather | solution.py:180
  128.9 0.3 convolution_convert_fusion.4
  129.2 0.7 scatter_fusion
  129.9 1.5 reshape.543
  131.4 0.4 convolution_bitcast_fusion
  131.9 2.2 %scatter_fusion.1 = f32[16,4,64,128]{3,2,1,0:T(8,128)} fusion(f32[16,4,64,128]{3,2,1,0:T(8,128)} %add_select_fusion, s32[2]{0:T(128)S(1)} %fusion.61, f32[2,4,64,128]{3,2,1,0:T(8,128)S(1)} %bitcast.108), kind=kCustom, calls=%fused_computation.12 | custom fusion | bytes 786440 | tf_op jit(solution)/shard_map/scatter | solution.py:194
  134.1 4.5 %reshape.545 = bf16[16,131072]{1,0:T(8,128)(2,1)} reshape(bf16[8,2,131072]{2,1,0:T(2,128)(2,1)} %all-gather.10.cloned.1.call-done) | data formatting | bytes 8388608
  138.6 3.1 %convolution_convert_fusion = bf16[2,131072]{1,0:T(2,128)(2,1)S(1)} fusion(bf16[16,131072]{1,0:T(8,128)(2,1)} %reshape.545, s32[16]{0:T(128)S(1)} %copy-done.15, pred[16]{0:T(512)(128)(4,1)S(1)} %copy-done.17), kind=kOutput, calls=%fused_computation.14 | convolution fusion | flops 8650816 | bytes 4718672 | tf_op jit(solution)/shard_map/dot_general | solution.py:89
  141.7 0.3 reshape.520
  142.0 2.5 %scatter_fusion.2 = bf16[16,4,128,256]{3,2,1,0:T(8,128)(2,1)} fusion(bf16[16,4,128,256]{3,2,1,0:T(8,128)(2,1)} %copy.118, s32[8]{0:T(128)S(1)} %reshape.518, bf16[8,128,256]{2,1,0:T(8,128)(2,1)S(1)} %reshape.520), kind=kCustom, calls=%fused_computation.13 | custom fusion | bytes 1572928 | tf_op jit(solution)/shard_map/scatter | solution.py:90
  (93 shorter events, 0.9 us)
Async XLA Ops:
  8.0 5.1 %copy-start = (bf16[1024,768]{1,0:T(8,128)(2,1)S(1)}, bf16[1024,768]{1,0:T(8,128)(2,1)}, u32[]{:S(2)}) copy-start(bf16[1024,768]{1,0:T(8,128)(2,1)} %param.31) | copy-start | bytes 4718596
  8.0 4.9 %copy-start.7 = (bf16[16,1024]{1,0:T(8,128)(2,1)S(1)}, bf16[16,1024]{1,0:T(8,128)(2,1)}, u32[]{:S(2)}) copy-start(bf16[16,1024]{1,0:T(8,128)(2,1)} %param.19) | copy-start | bytes 98308
  8.0 5.1 %copy-start.12 = (f32[1024]{0:T(1024)S(1)}, f32[1024]{0:T(1024)}, u32[]{:S(2)}) copy-start(f32[1024]{0:T(1024)} %param.29) | copy-start | bytes 12292
  8.0 88.2 %all-reduce.4.cloned.1.call-start = ((), (), s32[]{:S(2)}) async-start(), calls=%async_computation | async-start | bytes 131072 | tf_op jit(solution)/shard_map/psum | solution.py:156
  12.9 16.8 %copy-start.4 = (s32[16,2,1]{0,2,1:T(1,128)S(1)}, s32[16,2,1]{0,2,1:T(1,128)}, u32[]{:S(2)}) copy-start(s32[16,2,1]{0,2,1:T(1,128)} %param.25) | copy-start | bytes 388
  12.9 17.6 %copy-start.6 = (bf16[8,4,64,256]{3,2,1,0:T(8,128)(2,1)S(1)}, bf16[8,4,64,256]{3,2,1,0:T(8,128)(2,1)}, u32[]{:S(2)}) copy-start(bf16[8,4,64,256]{3,2,1,0:T(8,128)(2,1)} %param.27) | copy-start | bytes 3145732
  12.9 17.6 %copy-start.19 = (s32[16]{0:T(128)S(1)}, s32[16]{0:T(128)}, u32[]{:S(2)}) copy-start(s32[16]{0:T(128)} %param.21) | copy-start | bytes 196
  33.6 5.0 %copy-start.18 = (s32[16]{0:T(128)S(1)}, s32[16]{0:T(128)}, u32[]{:S(2)}) copy-start(s32[16]{0:T(128)} %param.20) | copy-start | bytes 196
  42.5 17.4 %collective-permute-start = (f32[16,4]{0,1:T(4,128)S(1)}, f32[16,4]{0,1:T(4,128)S(1)}, u32[]{:S(2)}, u32[]{:S(2)}) collective-permute-start(f32[16,4]{0,1:T(4,128)S(1)} %fusion.56), channel_id=1, source_target_pairs={{0,2},{2,0},{1,3},{3,1},{4,6},{6,4},{5,7},{7,5},{8,10},{10,8},{9,1... | collective-permute-start | bytes 776 | tf_op jit(solution)/shard_map/ppermute | solution.py:16
  43.9 7.8 %copy-start.3 = (f32[16,4,64,128]{3,2,1,0:T(8,128)S(1)}, f32[16,4,64,128]{3,2,1,0:T(8,128)}, u32[]{:S(2)}) copy-start(f32[16,4,64,128]{3,2,1,0:T(8,128)} %param.28) | copy-start | bytes 6291460
  48.6 11.3 %collective-permute-start.1 = (f32[16,4,128]{2,0,1:T(8,128)S(1)}, f32[16,4,128]{2,0,1:T(8,128)S(1)}, u32[]{:S(2)}, u32[]{:S(2)}) collective-permute-start(f32[16,4,128]{2,0,1:T(8,128)S(1)} %bitcast_add_fusion), channel_id=1, source_target_pairs={{0,2},{2,0},{1,3},{3,1},{4,6},{6,4},{5,7},{7,5},{8,10},{10,8},{9,1... | collective-permute-start | bytes 98312 | tf_op jit(solution)/shard_map/ppermute | solution.py:16
  50.9 8.9 %collective-permute-start.2 = (f32[16,4]{0,1:T(4,128)S(1)}, f32[16,4]{0,1:T(4,128)S(1)}, u32[]{:S(2)}, u32[]{:S(2)}) collective-permute-start(f32[16,4]{0,1:T(4,128)S(1)} %get-tuple-element.11), channel_id=1, source_target_pairs={{0,2},{2,0},{1,3},{3,1},{4,6},{6,4},{5,7},{7,5},{8,10},{10,8},{9,1... | collective-permute-start | bytes 776 | tf_op jit(solution)/shard_map/ppermute | solution.py:16
  51.7 6.8 %copy-start.20 = (s32[1,2]{1,0:T(1,128)S(1)}, s32[1,2]{1,0:T(1,128)}, u32[]{:S(2)}) copy-start(s32[1,2]{1,0:T(1,128)} %param.23) | copy-start | bytes 28
  51.7 6.8 %copy-start.21 = (s32[16]{0:T(128)S(1)}, s32[16]{0:T(128)}, u32[]{:S(2)}) copy-start(s32[16]{0:T(128)} %param.22) | copy-start | bytes 196
  51.7 6.8 %copy-start.1 = (f32[8]{0:T(128)S(1)}, f32[8]{0:T(128)}, u32[]{:S(2)}) copy-start(f32[8]{0:T(128)} %param.37) | copy-start | bytes 100
  51.7 7.5 %copy-start.2 = (f32[8]{0:T(128)S(1)}, f32[8]{0:T(128)}, u32[]{:S(2)}) copy-start(f32[8]{0:T(128)} %param.36) | copy-start | bytes 100
  55.1 5.1 %copy-start.10 = (bf16[256,1024]{1,0:T(8,128)(2,1)S(1)}, bf16[256,1024]{1,0:T(8,128)(2,1)}, u32[]{:S(2)}) copy-start(bf16[256,1024]{1,0:T(8,128)(2,1)} %param.32) | copy-start | bytes 1572868
  61.0 68.9 %all-gather.8.cloned.1.call-start = ((), (), s32[]{:S(2)}) async-start(), calls=%async_computation.1 | async-start | bytes 1179648 | tf_op jit(solution)/shard_map/all_gather | solution.py:183
  64.1 33.1 %copy-start.13 = (f32[1024]{0:T(1024)S(1)}, f32[1024]{0:T(1024)}, u32[]{:S(2)}) copy-start(f32[1024]{0:T(1024)} %param.30) | copy-start | bytes 12292
  64.1 34.0 %copy-start.5 = (bf16[1024,704]{0,1:T(8,128)(2,1)S(1)}, bf16[1024,704]{0,1:T(8,128)(2,1)}, u32[]{:S(2)}) copy-start(bf16[1024,704]{0,1:T(8,128)(2,1)} %param.33) | copy-start | bytes 4325380
  67.1 67.0 %all-gather.10.cloned.1.call-start = ((), (), s32[]{:S(2)}) async-start(), calls=%async_computation.2 | async-start | bytes 4718592 | tf_op jit(solution)/shard_map/all_gather | solution.py:87
  85.0 43.9 %copy-start.14 = (s32[16]{0:T(128)}, s32[16]{0:T(128)S(1)}, u32[]{:S(2)}) copy-start(s32[16]{0:T(128)S(1)} %and_select_fusion) | copy-start | bytes 196
  85.0 43.9 %copy-start.16 = (pred[16]{0:T(512)(128)(4,1)}, pred[16]{0:T(512)(128)(4,1)S(1)}, u32[]{:S(2)}) copy-start(pred[16]{0:T(512)(128)(4,1)S(1)} %broadcast_compare_fusion.1) | copy-start | bytes 52
  98.1 21.0 %copy-start.8 = (bf16[16,1024]{1,0:T(8,128)(2,1)S(1)}, bf16[16,1024]{1,0:T(8,128)(2,1)}, u32[]{:S(2)}) copy-start(bf16[16,1024]{1,0:T(8,128)(2,1)} %param.19) | copy-start | bytes 98308
  98.1 21.0 %copy-start.9 = (f32[16,1024]{1,0:T(8,128)S(1)}, f32[16,1024]{1,0:T(8,128)}, u32[]{:S(2)}) copy-start(f32[16,1024]{1,0:T(8,128)} %all-reduce.4.cloned.1.call-done) | copy-start | bytes 196612
  129.2 2.2 %copy-start.15 = (s32[16]{0:T(128)S(1)}, s32[16]{0:T(128)}, u32[]{:S(2)}) copy-start(s32[16]{0:T(128)} %copy-done.14) | copy-start | bytes 196
  129.2 2.2 %copy-start.17 = (pred[16]{0:T(512)(128)(4,1)S(1)}, pred[16]{0:T(512)(128)(4,1)}, u32[]{:S(2)}) copy-start(pred[16]{0:T(512)(128)(4,1)} %copy-done.16) | copy-start | bytes 52
  129.9 4.2 %copy-start.11 = (bf16[16,1024]{1,0:T(8,128)(2,1)}, bf16[16,1024]{1,0:T(8,128)(2,1)S(1)}, u32[]{:S(2)}) copy-start(bf16[16,1024]{1,0:T(8,128)(2,1)S(1)} %scatter_fusion) | copy-start | bytes 98308
Sparse Core Ops, SparseCore 0:
  61.1 35.0 all-reduce.3
Sparse Core Ops, SparseCore 1:
  67.1 24.4 all-gather.7
  93.5 36.6 all-gather.9
where the time goes:
time: 153 us; the launch traced here: 152 us
  blocking collectives  49.8 us (33%)
  local copies, waits for them, and re-layouts  38.9 us (25%)
  matrix products  24 us (16%)
  between operations  16.6 us (11%)
  waiting for transfers between devices  11.2 us (7%)
  other arithmetic  7.61 us (5%)
  starting transfers between devices  3.86 us (3%)
    psum x1, blocking collectives, body(): lax.psum(jnp.dot(activated, down_weight, preferred_element_type=jnp.float...  17.6 us
    all_gather x1, blocking collectives, body(): qkv_full = lax.all_gather(qkv_part, 'tp', axis=1, tiled=True)  15 us
    unnamed x55, local copies, waits for them, and re-layouts  14.6 us
    psum x1, waiting for transfers between devices, body(): hidden_in = residual_in + lax.psum(attn_term, 'tp')  11.2 us
    all_gather x1, blocking collectives, body(): lax.all_gather(send_rows.astype(jnp.bfloat16), 'rep', axis=0, tiled=True)  9.15 us
    unnamed x1, blocking collectives  8.01 us
    gather x1, local copies, waits for them, and re-layouts, body(): cache_pool[page_ids, sect_index]  4.95 us
    dot_general x1, matrix products, body(): jnp.einsum('rsn,rsnd->rsd', weights, key_data[..., head_dim:].astype(jnp....  4.54 us
  transfers between devices with their start and end apart: 6, of which 1 were waited for; matrix products, arithmetic and copies ran while one was open for 26% of the time, Pallas kernels for 0%

commit v1 on v0

v1 whole, which is shorter than its diff:
```python
import functools
import math

import jax
import jax.numpy as jnp
from jax import lax
from jax.experimental import pallas as pl
from jax.experimental.pallas import tpu as pltpu
from jax.sharding import PartitionSpec as P

MESH = pl.DeviceIdType.MESH
f32, bf16, i32 = jnp.float32, jnp.bfloat16, jnp.int32
LOW = -1e30


def split2(x):
    hi = x.astype(bf16)
    lo = (x - hi.astype(f32)).astype(bf16)
    return hi, lo


def dot_t(a, b):
    return lax.dot_general(a, b, (((1,), (1,)), ((), ())), preferred_element_type=f32)


def rms_scale(values, gain_vec):
    return values * lax.rsqrt(jnp.mean(values * values, axis=-1, keepdims=True) + 1e-05) * gain_vec


def unit_rows(values):
    return values * lax.rsqrt(jnp.sum(values * values, axis=-1, keepdims=True) + 1e-06)


def column(ref_values, count):
    rows = lax.broadcasted_iota(i32, (count, 1), 0)
    out = jnp.zeros((count, 1), i32)
    for r in range(count):
        out = jnp.where(rows == r, ref_values(r), out)
    return out


def step_kernel(
    n_rep, n_tp,
    lengths, group, span, out_slot, move_dest, table, forget, rate,
    norm_attn, norm_mlp, tokens_hbm, qkvw_hbm, pool_hbm, prefix_hbm, mem_hbm,
    outw_hbm, gatew_hbm, upw_hbm, downw_hbm,
    rows_out, mem_after, mem_in, pages_in,
    tokens, qkvw, pool, prefix, mem, outw, gatew, upw, downw, mem_new,
    qbuf, dtab, part_send, part_recv, ar_one, ar_two, row_buf, held_page, held_mem,
    pick_page, pick_mem,
    load_sem, out_sem, q_send, q_recv, d_send, d_recv, part_sem, one_send, one_recv,
    two_send, two_recv, row_send, row_recv, page_send, page_recv, mem_send, mem_recv,
):
    n_req, model_dim = tokens.shape
    n_pool, n_sect, page_len, width = pool.shape
    head_dim = width // 2
    n_group, _, pre_len, _ = prefix.shape
    half_dim = mem.shape[2]
    n_head = model_dim // head_dim
    n_move = out_slot.shape[1]
    n_block, _, block = qbuf.shape
    own_blocks = n_block // n_tp
    per_head = head_dim // block
    routed = n_rep == 8
    scale = head_dim ** (-0.5)
    rep = lax.axis_index("rep")
    tp = lax.axis_index("tp")
    half = (tp * n_sect) // n_head

    def rep_flip(bits):
        return rep + bits * (1 - 2 * (lax.rem(lax.div(rep, bits), 2)))

    loads = []
    for i, (src, dst) in enumerate([
        (tokens_hbm, tokens), (qkvw_hbm, qkvw), (pool_hbm, pool), (prefix_hbm, prefix),
        (mem_hbm, mem), (outw_hbm, outw), (gatew_hbm, gatew), (upw_hbm, upw), (downw_hbm, downw),
    ]):
        copy = pltpu.make_async_copy(src, dst, load_sem.at[i])
        copy.start()
        loads.append(copy)

    barrier = pltpu.get_barrier_semaphore()
    for o in range(1, n_tp):
        pl.semaphore_signal(
            barrier, inc=1, device_id=(rep, lax.rem(tp + o, n_tp)), device_id_type=MESH
        )
    for o in range(1, n_rep):
        pl.semaphore_signal(
            barrier, inc=1, device_id=(lax.rem(rep + o, n_rep), tp), device_id_type=MESH
        )

    def tp_gather(buf_own, send, recv):
        copies = []
        for o in range(1, n_tp):
            copy = pltpu.make_async_remote_copy(
                src_ref=buf_own, dst_ref=buf_own, send_sem=send.at[o - 1], recv_sem=recv.at[o - 1],
                device_id=(rep, lax.rem(tp + o, n_tp)), device_id_type=MESH,
            )
            copy.start()
            copies.append(copy)
        return copies

    def rep_gather(buf_own, send, recv):
        copies = []
        for o in range(1, n_rep):
            copy = pltpu.make_async_remote_copy(
                src_ref=buf_own, dst_ref=buf_own, send_sem=send.at[o - 1], recv_sem=recv.at[o - 1],
                device_id=(lax.rem(rep + o, n_rep), tp), device_id_type=MESH,
            )
            copy.start()
            copies.append(copy)
        return copies

    def wait_all(copies):
        for copy in copies:
            copy.wait()

    loads[0].wait()
    residual = tokens[...].astype(f32)
    normed = rms_scale(residual, norm_attn[...]).astype(bf16)
    lane = lax.broadcasted_iota(i32, (8, 128), 1)
    tags = jnp.zeros((8, 128), i32)
    for m in range(n_move):
        tags = jnp.where(lane == m, move_dest[0, m], tags)
    dtab[rep] = tags
    loads[1].wait()
    qkv = jnp.dot(normed, qkvw[...], preferred_element_type=f32).astype(bf16)
    for b in range(own_blocks):
        qbuf[tp * own_blocks + b] = qkv[:, b * block:(b + 1) * block]

    pl.semaphore_wait(barrier, n_tp + n_rep - 2)
    q_copies = tp_gather(qbuf.at[pl.ds(tp * own_blocks, own_blocks)], q_send, q_recv)
    d_copies = rep_gather(dtab.at[rep], d_send, d_recv)

    def push(src, dst, send, recv, peer):
        copy = pltpu.make_async_remote_copy(
            src_ref=src, dst_ref=dst, send_sem=send, recv_sem=recv,
            device_id=(peer, tp), device_id_type=MESH,
        )
        copy.start()
        return copy

    first_bits, last_bits = (2, 4), (4, 2)

    def route_begin(held, send, recv):
        if not routed:
            return rep_gather(held.at[rep], send, recv)
        copies = []
        for k in range(2):
            copies.append(push(held.at[k, 0], held.at[k, 2], send.at[k, 0], recv.at[k, 0],
                               rep_flip(first_bits[k])))
        for k in range(2):
            copies.append(push(held.at[k, 0], held.at[k, 1], send.at[k, 1], recv.at[k, 1],
                               rep_flip(1)))
        return copies

    def route_forward(copies, held, send, recv):
        if not routed:
            return
        for k in range(2):
            copies[k].wait_recv()
            copies.append(push(held.at[k, 2], held.at[k, 3], send.at[k, 2], recv.at[k, 2],
                               rep_flip(1)))

    def dest_of(r, m):
        return dtab[r][0:1, m:m + 1]

    def slot_rep(k, j):
        there = rep if j < 2 else rep_flip(first_bits[k])
        if j % 2:
            there = there + 1 - 2 * lax.rem(there, 2)
        return there

    def choose(held, k, m, s, wanted):
        out = held[k, 0, m, s].astype(f32)
        for j in range(1, 4):
            out = jnp.where(dest_of(slot_rep(k, j), m) == wanted, held[k, j, m, s].astype(f32), out)
        return out

    def route_last(copies, held, pick, send, recv):
        if not routed:
            return
        for copy in copies[2:6]:
            copy.wait_recv()
        for k in range(2):
            peer = rep_flip(last_bits[k])
            for m in range(n_move):
                for s in range(n_sect):
                    pick[k, m, s] = choose(held, k, m, s, peer).astype(bf16)
            copies.append(push(pick.at[k], held.at[k, 4], send.at[k, 3], recv.at[k, 3], peer))

    def route_end(copies, held, out_ref):
        if not routed:
            wait_all(copies)
            for m in range(n_move):
                for s in range(n_sect):
                    def body(r, acc):
                        return jnp.where(dest_of(r, m) == rep, held[r, m, s].astype(f32), acc)
                    out_ref[m, s] = lax.fori_loop(
                        0, n_rep, body, jnp.zeros(out_ref.shape[2:], f32)
                    ).astype(out_ref.dtype)
            return
        for copy in copies[6:8]:
            copy.wait_recv()
        for copy in copies:
            copy.wait_send()
        rows = held.shape[4]
        for k in range(2):
            for m in range(n_move):
                for s in range(n_sect):
                    out = held[k, 4, m, s].astype(f32)
                    for j in range(4):
                        out = jnp.where(dest_of(slot_rep(k, j), m) == rep,
                                        held[k, j, m, s].astype(f32), out)
                    out_ref[m, s, pl.ds(k * rows, rows)] = out.astype(out_ref.dtype)

    loads[2].wait()
    for m in range(n_move):
        page = table[out_slot[0, m], half]
        for s in range(n_sect):
            leaving = pool[page, s]
            if routed:
                cut = page_len // 2
                held_page[0, 0, m, s] = leaving[:cut]
                held_page[1, 0, m, s] = leaving[cut:]
            else:
                held_page[rep, m, s] = leaving
    page_copies = route_begin(held_page, page_send, page_recv)

    page_col = column(lambda r: table[r, half], n_req)
    length_col = column(lambda r: lengths[r], n_req)
    group_col = column(lambda r: group[r], n_req)
    span_col = column(lambda r: span[r], n_req)
    keys_at = lax.broadcasted_iota(i32, (n_req, n_pool * page_len), 1)
    live_pool = (keys_at // page_len == page_col) & (
        keys_at % page_len + half * page_len < length_col
    )
    pre_at = lax.broadcasted_iota(i32, (n_req, n_group * pre_len), 1)
    live_pre = pre_at // pre_len == group_col
    loads[3].wait()
    wait_all(q_copies)

    def head_rows(base, s):
        head = lax.rem(tp * n_sect + s, n_head)
        parts = [qbuf[base * n_head * per_head + head * per_head + j] for j in range(per_head)]
        return parts[0] if per_head == 1 else jnp.concatenate(parts, axis=1)

    queries = [head_rows(0, s) for s in range(n_sect)]
    new_keys = [head_rows(1, s).astype(f32) for s in range(n_sect)]
    new_values = [head_rows(2, s).astype(f32) for s in range(n_sect)]
    wide = lax.broadcasted_iota(i32, (n_req, 128), 1)
    stats = jnp.zeros((n_req, 128), f32)
    tops, denoms, accs = [], [], []
    for s in range(n_sect):
        q = queries[s]
        k_pool = pool[:, s, :, :head_dim].reshape(n_pool * page_len, head_dim)
        v_pool = pool[:, s, :, head_dim:].reshape(n_pool * page_len, head_dim)
        k_pre = prefix[:, s, :, :head_dim].reshape(n_group * pre_len, head_dim)
        v_pre = prefix[:, s, :, head_dim:].reshape(n_group * pre_len, head_dim)
        s_pool = jnp.where(live_pool, dot_t(q, k_pool) * scale, LOW)
        s_pre = jnp.where(live_pre, dot_t(q, k_pre) * scale, LOW)
        own = jnp.sum(q.astype(f32) * new_keys[s], axis=-1, keepdims=True) * scale
        own = jnp.where(half == 0, own, LOW)
        top = jnp.maximum(jnp.max(s_pool, axis=-1, keepdims=True),
                          jnp.max(s_pre, axis=-1, keepdims=True))
        top = jnp.maximum(top, own)
        w_pool = jnp.exp(s_pool - top)
        w_pre = jnp.exp(s_pre - top)
        w_own = jnp.exp(own - top)
        denom = (jnp.sum(w_pool, axis=-1, keepdims=True) + jnp.sum(w_pre, axis=-1, keepdims=True)
                 + w_own)
        both = jnp.dot(jnp.concatenate(split2(w_pool), axis=0), v_pool, preferred_element_type=f32)
        both = both + jnp.dot(
            jnp.concatenate(split2(w_pre), axis=0), v_pre, preferred_element_type=f32
        )
        acc = both[:n_req] + both[n_req:] + w_own * new_values[s]
        part_send[s] = acc
        stats = jnp.where(wide == s, top, stats)
        stats = jnp.where(wide == 64 + s, denom, stats)
        tops.append(top)
        denoms.append(denom)
        accs.append(acc)
    part_send[n_sect] = stats
    partner = lax.rem(tp + n_tp // 2, n_tp)
    part_copy = pltpu.make_async_remote_copy(
        src_ref=part_send, dst_ref=part_recv, send_sem=part_sem.at[0], recv_sem=part_sem.at[1],
        device_id=(rep, partner), device_id_type=MESH,
    )
    part_copy.start()

    loads[4].wait()
    mem_at = lax.broadcasted_iota(i32, (n_req, n_req * half_dim), 1)
    mem_row = lax.broadcasted_iota(i32, (n_req, n_req * half_dim), 0)
    mine = mem_at // half_dim == mem_row
    writes = mine & (span_col == 1)
    recalls = []

    def own_half(x):
        return jnp.where(half == 0, x[:, :half_dim], x[:, half_dim:])

    for s in range(n_sect):
        head = lax.rem(tp * n_sect + s, n_head)
        q_hi, q_lo = split2(unit_rows(queries[s].astype(f32)))
        k_hi, k_lo = split2(unit_rows(new_keys[s]))
        m_hi, m_lo = split2(mem[:, s].reshape(n_req * half_dim, head_dim))
        by_hi = dot_t(jnp.concatenate([q_hi, k_hi, q_lo, k_lo], axis=0), m_hi)
        by_lo = dot_t(jnp.concatenate([q_hi, k_hi], axis=0), m_lo)
        seen = by_hi[:2 * n_req] + by_hi[2 * n_req:] + by_lo
        recalled = jnp.where(mine, seen[:n_req], 0.0)
        fold = recalled[:, :128]
        for c in range(1, n_req * half_dim // 128):
            fold = fold + recalled[:, c * 128:(c + 1) * 128]
        recalls.append(fold[:, :half_dim] + fold[:, half_dim:])
        value = own_half(new_values[s])
        value = jnp.concatenate([value] * (n_req), axis=1)
        miss = jnp.where(writes, rate[head] * (value - seen[n_req:]), 0.0)
        miss_hi = miss.astype(bf16).astype(f32)
        stack = jnp.concatenate([miss_hi, miss - miss_hi, miss_hi], axis=0)
        grow = jnp.dot(
            jnp.transpose(stack).astype(bf16), jnp.concatenate([k_hi, k_hi, k_lo], axis=0),
            preferred_element_type=f32,
        )
        keep = forget[head]
        for r in range(n_req):
            kept = jnp.where(span[r] == 1, keep, 1.0)
            mem_new[r, s] = kept * mem[r, s] + grow[r * half_dim:(r + 1) * half_dim]
    mem_copy = pltpu.make_async_copy(mem_new, mem_after, out_sem)
    mem_copy.start()
    for m in range(n_move):
        for s in range(n_sect):
            leaving = mem_new[out_slot[0, m], s].astype(bf16)
            if routed:
                cut = half_dim // 2
                held_mem[0, 0, m, s] = leaving[:cut]
                held_mem[1, 0, m, s] = leaving[cut:]
            else:
                held_mem[rep, m, s] = leaving
    mem_copies = route_begin(held_mem, mem_send, mem_recv)

    part_copy.wait()
    theirs = part_recv[n_sect]
    mixed = []
    for s in range(n_sect):
        top_b = jnp.sum(jnp.where(wide == s, theirs, 0.0), axis=-1, keepdims=True)
        den_b = jnp.sum(jnp.where(wide == 64 + s, theirs, 0.0), axis=-1, keepdims=True)
        top = jnp.maximum(tops[s], top_b)
        w_a, w_b = jnp.exp(tops[s] - top), jnp.exp(top_b - top)
        total = accs[s] * w_a + part_recv[s] * w_b
        attended = total / (denoms[s] * w_a + den_b * w_b)
        mixed.append(own_half(attended) + recalls[s])
    mixed = mixed[0] if n_sect == 1 else jnp.concatenate(mixed, axis=1)
    loads[5].wait()
    ar_one[tp] = jnp.dot(mixed.astype(bf16), outw[...], preferred_element_type=f32).astype(bf16)
    one_copies = tp_gather(ar_one.at[tp], one_send, one_recv)
    wait_all(d_copies)
    route_forward(page_copies, held_page, page_send, page_recv)
    wait_all(one_copies)
    hidden = residual
    for t in range(n_tp):
        hidden = hidden + ar_one[t].astype(f32)
    normed = rms_scale(hidden, norm_mlp[...]).astype(bf16)
    loads[6].wait()
    gate = jnp.dot(normed, gatew[...], preferred_element_type=f32)
    loads[7].wait()
    up = jnp.dot(normed, upw[...], preferred_element_type=f32)
    activated = (gate * jax.nn.sigmoid(gate) * up).astype(bf16)
    loads[8].wait()
    ar_two[tp] = jnp.dot(activated, downw[...], preferred_element_type=f32).astype(bf16)
    two_copies = tp_gather(ar_two.at[tp], two_send, two_recv)
    route_last(page_copies, held_page, pick_page, page_send, page_recv)
    route_forward(mem_copies, held_mem, mem_send, mem_recv)
    wait_all(two_copies)
    total = ar_two[0].astype(f32)
    for t in range(1, n_tp):
        total = total + ar_two[t].astype(f32)
    rows = (hidden + total).astype(bf16)

    n_piece = model_dim // 128
    row_len = row_buf.shape[1]
    to_buf = lax.broadcasted_iota(i32, (row_len, n_req), 0)
    from_slot = lax.broadcasted_iota(i32, (row_len, n_req), 1)
    packed = jnp.zeros((row_len, 128), f32)
    for c in range(n_piece):
        hot = jnp.zeros((row_len, n_req), f32)
        for m in range(n_move):
            hot = jnp.where((to_buf == c * n_move + m) & (from_slot == out_slot[0, m]), 1.0, hot)
        packed = packed + jnp.dot(
            hot.astype(bf16), rows[:, c * 128:(c + 1) * 128], preferred_element_type=f32
        )
    row_buf[rep] = packed.astype(bf16)
    row_copies = rep_gather(row_buf.at[rep], row_send, row_recv)
    route_last(mem_copies, held_mem, pick_mem, mem_send, mem_recv)
    route_end(page_copies, held_page, pages_in)
    wait_all(row_copies)
    arrived = row_buf[...].reshape(n_rep * row_len, 128)
    slot_at = lax.broadcasted_iota(i32, (n_req, row_len), 0)
    buf_at = lax.broadcasted_iota(i32, (n_req, row_len), 1)
    slot_col = lax.broadcasted_iota(i32, (n_req, 1), 0)
    staying = jnp.ones((n_req, 1), jnp.bool_)
    for m in range(n_move):
        staying = staying & (slot_col != out_slot[0, m])
    chosen = jnp.zeros((row_len, 128), f32)
    buf_move = lax.broadcasted_iota(i32, (row_len, 128), 0) % n_move
    for r in range(n_rep):
        hit = jnp.zeros((row_len, 128), i32)
        for m in range(n_move):
            hit = jnp.where((buf_move == m) & (dest_of(r, m) == rep), 1, hit)
        chosen = jnp.where(hit == 1, row_buf[r].astype(f32), chosen)
    chosen = chosen.astype(bf16)
    for c in range(n_piece):
        hot = jnp.zeros((n_req, row_len), f32)
        for m in range(n_move):
            hot = jnp.where((buf_at == c * n_move + m) & (slot_at == out_slot[0, m]), 1.0, hot)
        came = jnp.dot(hot.astype(bf16), chosen, preferred_element_type=f32)
        kept = rows[:, c * 128:(c + 1) * 128].astype(f32)
        rows_out[:, c * 128:(c + 1) * 128] = jnp.where(staying, kept, came).astype(bf16)
    route_end(mem_copies, held_mem, mem_in)
    mem_copy.wait()


def place_kernel(
    table, out_slot, rows, pool, pages_in, mem, mem_in, rows_out, pool_out, mem_out,
    page_sem, mem_sem,
):
    n_pool, n_sect = pool.shape[0], pool.shape[1]
    n_req = mem.shape[0]
    n_head = rows.shape[1] // mem.shape[3]
    n_move = out_slot.shape[1]
    half = (lax.axis_index("tp") * n_sect) // n_head
    slots = [out_slot[0, m] for m in range(n_move)]
    pages = [table[slot, half] for slot in slots]

    def put(index, moved, kept, arrived, out, sem):
        stays = index >= 0
        for m in range(n_move):
            stays = stays & (index != moved[m])

            @pl.when(index == moved[m])
            def _(m=m):
                pltpu.make_async_copy(arrived.at[m], out.at[index], sem).start()

        @pl.when(stays)
        def _():
            pltpu.make_async_copy(kept.at[index], out.at[index], sem).start()

    for p in range(n_pool):
        put(jnp.int32(p), pages, pool, pages_in, pool_out, page_sem.at[p])
    for r in range(n_req):
        put(jnp.int32(r), slots, mem, mem_in, mem_out, mem_sem.at[r])
    rows_out[...] = rows[...]
    for p in range(n_pool):
        pltpu.make_async_copy(pool.at[p], pool_out.at[p], page_sem.at[p]).wait()
    for r in range(n_req):
        pltpu.make_async_copy(mem.at[r], mem_out.at[r], mem_sem.at[r]).wait()


def body(
    n_rep, n_tp, tokens, lengths, prompt_group, span_close, out_slot, move_dest, page_table,
    cache_pool, prefix_cache, memory, norm_attn, norm_mlp, qkv_weight, out_weight, gate_weight,
    up_weight, down_weight, forget, write_rate,
):
    n_req, model_dim = tokens.shape
    n_pool, n_sect, page_len, width = cache_pool.shape
    half_dim, head_dim = memory.shape[2:]
    n_move = out_slot.shape[1]
    columns = qkv_weight.shape[1]
    block = math.gcd(columns, head_dim)
    row_len = n_move * model_dim // 128
    table = page_table[:, :, 0]
    smem = pl.BlockSpec(memory_space=pltpu.SMEM)
    vmem = pl.BlockSpec(memory_space=pltpu.VMEM)
    anym = pl.BlockSpec(memory_space=pl.ANY)
    if n_rep == 8:
        lead, moved_sems = (2, 5), (2, 4)
        page_piece = (n_move, n_sect, page_len // 2, width)
        mem_piece = (n_move, n_sect, half_dim // 2, head_dim)
        picks = (2,)
    else:
        lead, moved_sems = (n_rep,), (n_rep - 1,)
        page_piece = (n_move, n_sect, page_len, width)
        mem_piece = (n_move, n_sect, half_dim, head_dim)
        picks = ()
    page_pick = picks + page_piece if picks else (8, 128)
    mem_pick = picks + mem_piece if picks else (8, 128)
    V, dma = pltpu.VMEM, pltpu.SemaphoreType.DMA
    whole = [tokens, qkv_weight, cache_pool, prefix_cache, memory, out_weight, gate_weight,
             up_weight, down_weight]
    rows, mem_after, mem_in, pages_in = pl.pallas_call(
        functools.partial(step_kernel, n_rep, n_tp),
        out_shape=(
            jax.ShapeDtypeStruct((n_req, model_dim), bf16),
            jax.ShapeDtypeStruct(memory.shape, f32),
            jax.ShapeDtypeStruct((n_move,) + memory.shape[1:], f32),
            jax.ShapeDtypeStruct((n_move,) + cache_pool.shape[1:], bf16),
        ),
        in_specs=[smem] * 8 + [vmem] * 2 + [anym] * 9,
        out_specs=(vmem, anym, vmem, vmem),
        scratch_shapes=[V(a.shape, a.dtype) for a in whole] + [
            V(memory.shape, f32),
            V((n_tp * columns // block, n_req, block), bf16),
            V((n_rep, 8, 128), i32),
            V((n_sect + 1, n_req, 128), f32),
            V((n_sect + 1, n_req, 128), f32),
            V((n_tp, n_req, model_dim), bf16),
            V((n_tp, n_req, model_dim), bf16),
            V((n_rep, row_len, 128), bf16),
            V(lead + page_piece, bf16),
            V(lead + mem_piece, bf16),
            V(page_pick, bf16),
            V(mem_pick, bf16),
            dma((9,)), dma,
            dma((n_tp - 1,)), dma((n_tp - 1,)),
            dma((n_rep - 1,)), dma((n_rep - 1,)),
            dma((2,)),
            dma((n_tp - 1,)), dma((n_tp - 1,)),
            dma((n_tp - 1,)), dma((n_tp - 1,)),
            dma((n_rep - 1,)), dma((n_rep - 1,)),
            dma(moved_sems), dma(moved_sems),
            dma(moved_sems), dma(moved_sems),
        ],
        compiler_params=pltpu.CompilerParams(
            collective_id=0, has_side_effects=True, vmem_limit_bytes=48 * 1024 * 1024
        ),
        name="step",
    )(lengths, prompt_group, span_close, out_slot, move_dest, table, forget, write_rate,
      norm_attn.reshape(1, model_dim), norm_mlp.reshape(1, model_dim), *whole)
    return pl.pallas_call(
        place_kernel,
        out_shape=(
            jax.ShapeDtypeStruct(rows.shape, bf16),
            jax.ShapeDtypeStruct(cache_pool.shape, bf16),
            jax.ShapeDtypeStruct(memory.shape, f32),
        ),
        in_specs=[smem] * 2 + [vmem] + [anym] * 4,
        out_specs=(vmem, anym, anym),
        scratch_shapes=[dma((n_pool,)), dma((n_req,))],
        name="place",
    )(table, out_slot, rows, cache_pool, pages_in, mem_after, mem_in)


def solution(mesh):
    row = P("rep", None)
    grid = P("rep", "tp", None, None)
    placed = (
        row, P("rep"), P("rep"), P("rep"), row, row, P("rep", None, None), grid,
        P(None, "tp", None, None), grid, P(), P(), P(None, "tp"), P("tp", None), P(None, "tp"),
        P(None, "tp"), P("tp", None), P(), P(),
    )

    def run(*args):
        rows, pool, mem = body(mesh.shape["rep"], mesh.shape["tp"], *args)
        return rows, mem, pool

    return jax.shard_map(
        run, mesh=mesh, in_specs=placed, out_specs=(row, grid, grid), check_vma=False
    )
```

time: 153 us -> 242 us (1.58)
  Pallas kernels: 0 us -> 226 us
  blocking collectives: 49.8 us -> 0 us
  local copies, waits for them, and re-layouts: 38.9 us -> 14.8 us
  matrix products: 24 us -> 0 us
  between operations: 16.6 us -> 0.7 us
  waiting for transfers between devices: 11.2 us -> 0 us
  other arithmetic: 7.61 us -> 0 us
  starting transfers between devices: 3.86 us -> 0 us
    pallas_call x0 -> x2, Pallas kernels: none -> 226 us  [the longest x1 193 us: body(): pl.pallas_call(place_kernel, out_shape=(jax.ShapeDtypeStruct(rows.shape,...]
    all_gather x2 -> x0, blocking collectives: 24.2 us -> none  [the longest x1 15 us: body(): qkv_full = lax.all_gather(qkv_part, 'tp', axis=1, tiled=True)]
    dot_general x12 -> x0, matrix products: 24 us -> none  [the longest x1 4.54 us: body(): jnp.einsum('rsn,rsnd->rsd', weights, key_data[..., head_dim:].astype(jnp....]
    psum x1 -> x0, blocking collectives: 17.6 us -> none  [body(): lax.psum(jnp.dot(activated, down_weight, preferred_element_type=jnp.float...]
    gather x12 -> x0, local copies, waits for them, and re-layouts: 14.7 us -> none  [the longest x1 4.95 us: body(): cache_pool[page_ids, sect_index]]
    psum x1 -> x0, waiting for transfers between devices: 11.2 us -> none  [body(): hidden_in = residual_in + lax.psum(attn_term, 'tp')]
    unnamed x1 -> x0, blocking collectives: 8.01 us -> none
    scatter x3 -> x0, local copies, waits for them, and re-layouts: 5.41 us -> none  [the longest x1 2.51 us: body(): cache_pool.at[slot_pages, sect_index]]
  transfers between devices with their start and end apart: 6 -> 0, of which waited for: 1 -> 0; matrix products, arithmetic and copies ran while one was open for 26% -> 0% of each run, Pallas kernels for 0% -> 0%
where the time goes in v1:
time: 242 us
  Pallas kernels  226 us (93%)
  local copies, waits for them, and re-layouts  14.8 us (6%)
    pallas_call x1, Pallas kernels, body(): pl.pallas_call(place_kernel, out_shape=(jax.ShapeDtypeStruct(rows.shape,...  193 us
    pallas_call x1, Pallas kernels, body(): pl.pallas_call(functools.partial(step_kernel, n_rep, n_tp), out_shape=(ja...  32.9 us
    unnamed x38, local copies, waits for them, and re-layouts  14 us

profile of v1, /device:TPU:0, one launch (start us, length us, event | category | flops | bytes accessed | tf_op | source)
XLA Modules:
  0.0 241.7 jit_solution(15425143471808138021)
XLA Ops:
  0.6 0.8 copy.25.table
  1.4 0.0 copy-start.6
  1.4 0.0 copy-start.4
  1.4 0.0 copy-start.9
  1.4 0.0 copy-start.10
  1.4 2.6 %copy.23.gatew_hbm = bf16[1024,704]{1,0:T(8,128)(2,1)} copy(bf16[1024,704]{0,1:T(8,128)(2,1)} %param.33) | data formatting | bytes 2883584 | tf_op args[14]
  4.0 0.0 copy-start
  4.0 0.0 copy-start.1
  4.0 2.7 %copy.24.upw_hbm = bf16[1024,704]{1,0:T(8,128)(2,1)} copy(bf16[1024,704]{0,1:T(8,128)(2,1)} %param.34) | data formatting | bytes 2883584 | tf_op args[15]
  6.7 0.0 copy-done.6
  6.7 0.0 copy-done.4
  6.7 0.0 copy-done.9
  6.7 0.0 copy-done.10
  6.7 0.0 copy-done
  6.8 0.0 copy-done.1
  6.8 0.0 copy-start.2
  6.8 1.2 copy-done.2
  8.0 0.0 copy-start.8
  8.0 0.8 copy-done.8
  8.8 0.0 copy-start.11
  8.8 0.7 copy-done.11
  9.4 0.0 copy-start.12
  9.4 0.7 copy-done.12
  10.1 0.0 copy-start.13
  10.1 0.7 copy-done.13
  10.7 0.0 copy-start.14
  10.7 0.7 copy-done.14
  11.4 0.0 copy-start.15
  11.4 0.7 copy-done.15
  12.0 0.0 copy-start.16
  12.0 0.7 copy-done.16
  12.7 0.0 copy-start.17
  12.7 0.7 copy-done.17
  13.3 32.9 %step.1 = (bf16[16,1024]{1,0:T(8,128)(2,1)S(1)}, f32[16,4,64,128]{3,2,1,0:T(8,128)}, f32[2,4,64,128]{3,2,1,0:T(8,128)S(1)}, bf16[2,4,128,256]{3,2,1,0:T(8,128)(2,1)S(1)}) custom-call(s32[16]{0:T(128)S(1)} %copy-done.12, s32[16]{0:T(128)S(1)} %copy-done.13, s32[16]{0:T(128)S(1)} %copy-done.14, s32[1,2]{1,0:T(1,128)S(1)} %copy-done.11, s32[1,2]{1,0:T(1,128)S(1)} %copy-done.15, ...), custom_call_target="tpu_custom_call" | custom-call | tf_op jit(solution)/shard_map/step/pallas_call | solution.py:488
  46.2 0.0 copy-start.3
  46.2 0.8 copy-done.3
  47.0 0.0 copy-start.5
  47.0 0.7 copy-done.5
  47.7 0.0 copy-start.7
  47.7 0.6 copy-done.7
  48.3 193.4 %place.1 = (bf16[16,1024]{1,0:T(8,128)(2,1)}, bf16[16,4,128,256]{3,2,1,0:T(8,128)(2,1)}, f32[16,4,64,128]{3,2,1,0:T(8,128)}) custom-call(s32[16,2]{1,0:T(8,128)} %copy-done.6, s32[1,2]{1,0:T(1,128)} %out_slot.3, bf16[16,1024]{1,0:T(8,128)(2,1)} %copy-done.7, bf16[16,4,128,256]{3,2,1,0:T(8,128)(2,1)} %pool.1, bf16[2,4,128,256]{3,2,1,0:T(8,128)(2,1)} %copy-done.3, ...), custom_call_target="tpu_custom_call" | custom-call | tf_op jit(solution)/shard_map/place/pallas_call | solution.py:527
Async XLA Ops:
  1.4 5.3 %copy-start.6 = (s32[16,2]{1,0:T(8,128)}, s32[16,2]{1,0:T(8,128)S(1)}, u32[]{:S(2)}) copy-start(s32[16,2]{1,0:T(8,128)S(1)} %copy.25.table) | copy-start | bytes 388
  1.4 5.3 %copy-start.4 = (bf16[256,1024]{1,0:T(8,128)(2,1)S(1)}, bf16[256,1024]{1,0:T(8,128)(2,1)}, u32[]{:S(2)}) copy-start(bf16[256,1024]{1,0:T(8,128)(2,1)} %outw_hbm.1) | copy-start | bytes 1572868
  1.4 5.3 %copy-start.9 = (f32[1024]{0:T(1024)S(1)}, f32[1024]{0:T(1024)}, u32[]{:S(2)}) copy-start(f32[1024]{0:T(1024)} %param.29) | copy-start | bytes 12292
  1.4 5.3 %copy-start.10 = (f32[1024]{0:T(1024)S(1)}, f32[1024]{0:T(1024)}, u32[]{:S(2)}) copy-start(f32[1024]{0:T(1024)} %param.30) | copy-start | bytes 12292
  4.0 2.7 %copy-start = (bf16[1024,768]{1,0:T(8,128)(2,1)S(1)}, bf16[1024,768]{1,0:T(8,128)(2,1)}, u32[]{:S(2)}) copy-start(bf16[1024,768]{1,0:T(8,128)(2,1)} %qkvw_hbm.1) | copy-start | bytes 4718596
  4.0 2.7 %copy-start.1 = (bf16[704,1024]{1,0:T(8,128)(2,1)S(1)}, bf16[704,1024]{1,0:T(8,128)(2,1)}, u32[]{:S(2)}) copy-start(bf16[704,1024]{1,0:T(8,128)(2,1)} %downw_hbm.1) | copy-start | bytes 4325380
  6.8 1.2 copy-start.2
  8.0 0.8 copy-start.8
  8.8 0.7 copy-start.11
  9.4 0.7 copy-start.12
  10.1 0.7 copy-start.13
  10.7 0.7 copy-start.14
  11.4 0.7 copy-start.15
  12.0 0.7 copy-start.16
  12.7 0.7 copy-start.17
  46.2 0.8 copy-start.3
  47.0 0.7 copy-start.5
  47.7 0.6 copy-start.7

commit v2 on v1

--- a/solution.py
+++ b/solution.py
@@ -11,6 +11,7 @@
 MESH = pl.DeviceIdType.MESH
 f32, bf16, i32 = jnp.float32, jnp.bfloat16, jnp.int32
 LOW = -1e30
+VMEM_BYTES = 64 * 1024 * 1024
 
 
 def split2(x):
@@ -41,14 +42,15 @@
 
 def step_kernel(
     n_rep, n_tp,
-    lengths, group, span, out_slot, move_dest, table, forget, rate,
-    norm_attn, norm_mlp, tokens_hbm, qkvw_hbm, pool_hbm, prefix_hbm, mem_hbm,
+    lengths_hbm, group_hbm, span_hbm, out_slot_hbm, move_dest_hbm, table_hbm, forget_hbm,
+    rate_hbm, norm_attn_hbm, norm_mlp_hbm, tokens_hbm, qkvw_hbm, pool_hbm, prefix_hbm, mem_hbm,
     outw_hbm, gatew_hbm, upw_hbm, downw_hbm,
     rows_out, mem_after, mem_in, pages_in,
-    tokens, qkvw, pool, prefix, mem, outw, gatew, upw, downw, mem_new,
+    lengths, group, span, out_slot, move_dest, table, forget, rate,
+    norm_attn, norm_mlp, tokens, qkvw, pool, prefix, mem, outw, gatew, upw, downw, mem_new,
     qbuf, dtab, part_send, part_recv, ar_one, ar_two, row_buf, held_page, held_mem,
     pick_page, pick_mem,
-    load_sem, out_sem, q_send, q_recv, d_send, d_recv, part_sem, one_send, one_recv,
+    small_sem, load_sem, out_sem, q_send, q_recv, d_send, d_recv, part_sem, one_send, one_recv,
     two_send, two_recv, row_send, row_recv, page_send, page_recv, mem_send, mem_recv,
 ):
     n_req, model_dim = tokens.shape
@@ -70,6 +72,15 @@
     def rep_flip(bits):
         return rep + bits * (1 - 2 * (lax.rem(lax.div(rep, bits), 2)))
 
+    smalls = []
+    for i, (src, dst) in enumerate([
+        (norm_attn_hbm, norm_attn), (move_dest_hbm, move_dest), (out_slot_hbm, out_slot),
+        (table_hbm, table), (lengths_hbm, lengths), (group_hbm, group), (span_hbm, span),
+        (forget_hbm, forget), (rate_hbm, rate), (norm_mlp_hbm, norm_mlp),
+    ]):
+        copy = pltpu.make_async_copy(src, dst, small_sem.at[i])
+        copy.start()
+        smalls.append(copy)
     loads = []
     for i, (src, dst) in enumerate([
         (tokens_hbm, tokens), (qkvw_hbm, qkvw), (pool_hbm, pool), (prefix_hbm, prefix),
@@ -115,6 +126,7 @@
         for copy in copies:
             copy.wait()
 
+    wait_all(smalls)
     loads[0].wait()
     residual = tokens[...].astype(f32)
     normed = rms_scale(residual, norm_attn[...]).astype(bf16)
@@ -216,7 +228,7 @@
 
     loads[2].wait()
     for m in range(n_move):
-        page = table[out_slot[0, m], half]
+        page = table[half, out_slot[0, m]]
         for s in range(n_sect):
             leaving = pool[page, s]
             if routed:
@@ -227,7 +239,7 @@
                 held_page[rep, m, s] = leaving
     page_copies = route_begin(held_page, page_send, page_recv)
 
-    page_col = column(lambda r: table[r, half], n_req)
+    page_col = column(lambda r: table[half, r], n_req)
     length_col = column(lambda r: lengths[r], n_req)
     group_col = column(lambda r: group[r], n_req)
     span_col = column(lambda r: span[r], n_req)
@@ -293,13 +305,12 @@
     mem_row = lax.broadcasted_iota(i32, (n_req, n_req * half_dim), 0)
     mine = mem_at // half_dim == mem_row
     writes = mine & (span_col == 1)
-    recalls = []
+    recalls, predicts, units = [], [], []
 
     def own_half(x):
         return jnp.where(half == 0, x[:, :half_dim], x[:, half_dim:])
 
     for s in range(n_sect):
-        head = lax.rem(tp * n_sect + s, n_head)
         q_hi, q_lo = split2(unit_rows(queries[s].astype(f32)))
         k_hi, k_lo = split2(unit_rows(new_keys[s]))
         m_hi, m_lo = split2(mem[:, s].reshape(n_req * half_dim, head_dim))
@@ -311,9 +322,33 @@
         for c in range(1, n_req * half_dim // 128):
             fold = fold + recalled[:, c * 128:(c + 1) * 128]
         recalls.append(fold[:, :half_dim] + fold[:, half_dim:])
-        value = own_half(new_values[s])
-        value = jnp.concatenate([value] * (n_req), axis=1)
-        miss = jnp.where(writes, rate[head] * (value - seen[n_req:]), 0.0)
+        predicts.append(seen[n_req:])
+        units.append((k_hi, k_lo))
+    wait_all(d_copies)
+    route_forward(page_copies, held_page, page_send, page_recv)
+
+    part_copy.wait()
+    theirs = part_recv[n_sect]
+    mixed = []
+    for s in range(n_sect):
+        top_b = jnp.sum(jnp.where(wide == s, theirs, 0.0), axis=-1, keepdims=True)
+        den_b = jnp.sum(jnp.where(wide == 64 + s, theirs, 0.0), axis=-1, keepdims=True)
+        top = jnp.maximum(tops[s], top_b)
+        w_a, w_b = jnp.exp(tops[s] - top), jnp.exp(top_b - top)
+        total = accs[s] * w_a + part_recv[s] * w_b
+        attended = total / (denoms[s] * w_a + den_b * w_b)
+        mixed.append(own_half(attended) + recalls[s])
+    mixed = mixed[0] if n_sect == 1 else jnp.concatenate(mixed, axis=1)
+    loads[5].wait()
+    ar_one[tp] = jnp.dot(mixed.astype(bf16), outw[...], preferred_element_type=f32).astype(bf16)
+    one_copies = tp_gather(ar_one.at[tp], one_send, one_recv)
+    route_last(page_copies, held_page, pick_page, page_send, page_recv)
+
+    for s in range(n_sect):
+        head = lax.rem(tp * n_sect + s, n_head)
+        k_hi, k_lo = units[s]
+        value = jnp.concatenate([own_half(new_values[s])] * n_req, axis=1)
+        miss = jnp.where(writes, rate[head] * (value - predicts[s]), 0.0)
         miss_hi = miss.astype(bf16).astype(f32)
         stack = jnp.concatenate([miss_hi, miss - miss_hi, miss_hi], axis=0)
         grow = jnp.dot(
@@ -336,38 +371,19 @@
             else:
                 held_mem[rep, m, s] = leaving
     mem_copies = route_begin(held_mem, mem_send, mem_recv)
-
-    part_copy.wait()
-    theirs = part_recv[n_sect]
-    mixed = []
-    for s in range(n_sect):
-        top_b = jnp.sum(jnp.where(wide == s, theirs, 0.0), axis=-1, keepdims=True)
-        den_b = jnp.sum(jnp.where(wide == 64 + s, theirs, 0.0), axis=-1, keepdims=True)
-        top = jnp.maximum(tops[s], top_b)
-        w_a, w_b = jnp.exp(tops[s] - top), jnp.exp(top_b - top)
-        total = accs[s] * w_a + part_recv[s] * w_b
-        attended = total / (denoms[s] * w_a + den_b * w_b)
-        mixed.append(own_half(attended) + recalls[s])
-    mixed = mixed[0] if n_sect == 1 else jnp.concatenate(mixed, axis=1)
-    loads[5].wait()
-    ar_one[tp] = jnp.dot(mixed.astype(bf16), outw[...], preferred_element_type=f32).astype(bf16)
-    one_copies = tp_gather(ar_one.at[tp], one_send, one_recv)
-    wait_all(d_copies)
-    route_forward(page_copies, held_page, page_send, page_recv)
     wait_all(one_copies)
     hidden = residual
     for t in range(n_tp):
         hidden = hidden + ar_one[t].astype(f32)
     normed = rms_scale(hidden, norm_mlp[...]).astype(bf16)
     loads[6].wait()
-    gate = jnp.dot(normed, gatew[...], preferred_element_type=f32)
+    gate = dot_t(normed, gatew[...])
     loads[7].wait()
-    up = jnp.dot(normed, upw[...], preferred_element_type=f32)
+    up = dot_t(normed, upw[...])
     activated = (gate * jax.nn.sigmoid(gate) * up).astype(bf16)
     loads[8].wait()
     ar_two[tp] = jnp.dot(activated, downw[...], preferred_element_type=f32).astype(bf16)
     two_copies = tp_gather(ar_two.at[tp], two_send, two_recv)
-    route_last(page_copies, held_page, pick_page, page_send, page_recv)
     route_forward(mem_copies, held_mem, mem_send, mem_recv)
     wait_all(two_copies)
     total = ar_two[0].astype(f32)
@@ -419,39 +435,55 @@
 
 
 def place_kernel(
-    table, out_slot, rows, pool, pages_in, mem, mem_in, rows_out, pool_out, mem_out,
-    page_sem, mem_sem,
+    table_hbm, out_slot_hbm, rows_hbm, pool, pages_in, mem, mem_in, rows_out, pool_out, mem_out,
+    table, out_slot, page_buf, mem_buf, small_sem, page_load, mem_load, page_sem, mem_sem,
 ):
+    smalls = [
+        pltpu.make_async_copy(table_hbm, table, small_sem.at[0]),
+        pltpu.make_async_copy(out_slot_hbm, out_slot, small_sem.at[1]),
+        pltpu.make_async_copy(rows_hbm, rows_out, small_sem.at[2]),
+    ]
+    for copy in smalls:
+        copy.start()
     n_pool, n_sect = pool.shape[0], pool.shape[1]
     n_req = mem.shape[0]
-    n_head = rows.shape[1] // mem.shape[3]
+    n_head = rows_hbm.shape[1] // mem.shape[3]
     n_move = out_slot.shape[1]
     half = (lax.axis_index("tp") * n_sect) // n_head
+    for copy in smalls[:2]:
+        copy.wait()
     slots = [out_slot[0, m] for m in range(n_move)]
-    pages = [table[slot, half] for slot in slots]
-
-    def put(index, moved, kept, arrived, out, sem):
+    pages = [table[half, slot] for slot in slots]
+
+    def fetch(index, moved, kept, arrived, buf, sem):
         stays = index >= 0
         for m in range(n_move):
             stays = stays & (index != moved[m])
 
             @pl.when(index == moved[m])
             def _(m=m):
-                pltpu.make_async_copy(arrived.at[m], out.at[index], sem).start()
+                pltpu.make_async_copy(arrived.at[m], buf.at[index], sem).start()
 
         @pl.when(stays)
         def _():
-            pltpu.make_async_copy(kept.at[index], out.at[index], sem).start()
+            pltpu.make_async_copy(kept.at[index], buf.at[index], sem).start()
 
     for p in range(n_pool):
-        put(jnp.int32(p), pages, pool, pages_in, pool_out, page_sem.at[p])
+        fetch(jnp.int32(p), pages, pool, pages_in, page_buf, page_load.at[p])
     for r in range(n_req):
-        put(jnp.int32(r), slots, mem, mem_in, mem_out, mem_sem.at[r])
-    rows_out[...] = rows[...]
+        fetch(jnp.int32(r), slots, mem, mem_in, mem_buf, mem_load.at[r])
+    outs = []
     for p in range(n_pool):
-        pltpu.make_async_copy(pool.at[p], pool_out.at[p], page_sem.at[p]).wait()
+        pltpu.make_async_copy(pool.at[p], page_buf.at[p], page_load.at[p]).wait()
+        outs.append(pltpu.make_async_copy(page_buf.at[p], pool_out.at[p], page_sem.at[p]))
+        outs[-1].start()
     for r in range(n_req):
-        pltpu.make_async_copy(mem.at[r], mem_out.at[r], mem_sem.at[r]).wait()
+        pltpu.make_async_copy(mem.at[r], mem_buf.at[r], mem_load.at[r]).wait()
+        outs.append(pltpu.make_async_copy(mem_buf.at[r], mem_out.at[r], mem_sem.at[r]))
+        outs[-1].start()
+    smalls[2].wait()
+    for copy in outs:
+        copy.wait()
 
 
 def body(
@@ -466,10 +498,9 @@
     columns = qkv_weight.shape[1]
     block = math.gcd(columns, head_dim)
     row_len = n_move * model_dim // 128
-    table = page_table[:, :, 0]
-    smem = pl.BlockSpec(memory_space=pltpu.SMEM)
+    table = page_table[:, :, 0].T
     vmem = pl.BlockSpec(memory_space=pltpu.VMEM)
-    anym = pl.BlockSpec(memory_space=pl.ANY)
+    hbm = pl.BlockSpec(memory_space=pltpu.HBM)
     if n_rep == 8:
         lead, moved_sems = (2, 5), (2, 4)
         page_piece = (n_move, n_sect, page_len // 2, width)
@@ -483,8 +514,10 @@
     page_pick = picks + page_piece if picks else (8, 128)
     mem_pick = picks + mem_piece if picks else (8, 128)
     V, dma = pltpu.VMEM, pltpu.SemaphoreType.DMA
-    whole = [tokens, qkv_weight, cache_pool, prefix_cache, memory, out_weight, gate_weight,
-             up_weight, down_weight]
+    small = [lengths, prompt_group, span_close, out_slot, move_dest, table, forget, write_rate]
+    gains = [norm_attn.reshape(1, model_dim), norm_mlp.reshape(1, model_dim)]
+    whole = [tokens, qkv_weight, cache_pool, prefix_cache, memory, out_weight, gate_weight.T,
+             up_weight.T, down_weight]
     rows, mem_after, mem_in, pages_in = pl.pallas_call(
         functools.partial(step_kernel, n_rep, n_tp),
         out_shape=(
@@ -493,10 +526,11 @@
             jax.ShapeDtypeStruct((n_move,) + memory.shape[1:], f32),
             jax.ShapeDtypeStruct((n_move,) + cache_pool.shape[1:], bf16),
         ),
-        in_specs=[smem] * 8 + [vmem] * 2 + [anym] * 9,
-        out_specs=(vmem, anym, vmem, vmem),
-        scratch_shapes=[V(a.shape, a.dtype) for a in whole] + [
-            V(memory.shape, f32),
+        in_specs=[hbm] * 19,
+        out_specs=(vmem, hbm, vmem, vmem),
+        scratch_shapes=[pltpu.SMEM(a.shape, a.dtype) for a in small] + [
+            V(a.shape, a.dtype) for a in gains + whole + [memory]
+        ] + [
             V((n_tp * columns // block, n_req, block), bf16),
             V((n_rep, 8, 128), i32),
             V((n_sect + 1, n_req, 128), f32),
@@ -508,7 +542,7 @@
             V(lead + mem_piece, bf16),
             V(page_pick, bf16),
             V(mem_pick, bf16),
-            dma((9,)), dma,
+            dma((10,)), dma((9,)), dma,
             dma((n_tp - 1,)), dma((n_tp - 1,)),
             dma((n_rep - 1,)), dma((n_rep - 1,)),
             dma((2,)),
@@ -519,11 +553,10 @@
             dma(moved_sems), dma(moved_sems),
         ],
         compiler_params=pltpu.CompilerParams(
-            collective_id=0, has_side_effects=True, vmem_limit_bytes=48 * 1024 * 1024
+            collective_id=0, has_side_effects=True, vmem_limit_bytes=VMEM_BYTES
         ),
         name="step",
-    )(lengths, prompt_group, span_close, out_slot, move_dest, table, forget, write_rate,
-      norm_attn.reshape(1, model_dim), norm_mlp.reshape(1, model_dim), *whole)
+    )(*small, *gains, *whole)
     return pl.pallas_call(
         place_kernel,
         out_shape=(
@@ -531,9 +564,14 @@
             jax.ShapeDtypeStruct(cache_pool.shape, bf16),
             jax.ShapeDtypeStruct(memory.shape, f32),
         ),
-        in_specs=[smem] * 2 + [vmem] + [anym] * 4,
-        out_specs=(vmem, anym, anym),
-        scratch_shapes=[dma((n_pool,)), dma((n_req,))],
+        in_specs=[hbm] * 7,
+        out_specs=(vmem, hbm, hbm),
+        scratch_shapes=[
+            pltpu.SMEM(table.shape, i32), pltpu.SMEM(out_slot.shape, i32),
+            V(cache_pool.shape, bf16), V(memory.shape, f32),
+            dma((3,)), dma((n_pool,)), dma((n_req,)), dma((n_pool,)), dma((n_req,)),
+        ],
+        compiler_params=pltpu.CompilerParams(vmem_limit_bytes=VMEM_BYTES),
         name="place",
     )(table, out_slot, rows, cache_pool, pages_in, mem_after, mem_in)
 

time: 242 us -> 41.9 us (0.17)
  Pallas kernels: 226 us -> 41.1 us
  local copies, waits for them, and re-layouts: 14.8 us -> 0 us
    pallas_call x1, Pallas kernels: 193 us -> 7.01 us  [body(): pl.pallas_call(place_kernel, out_shape=(jax.ShapeDtypeStruct(rows.shape,...]
    unnamed x38 -> x0, local copies, waits for them, and re-layouts: 14 us -> none
where the time goes in v2:
time: 41.9 us; the launch traced here: 41.7 us
  Pallas kernels  41.1 us (98%)
  between operations  0.65 us (2%)
    pallas_call x1, Pallas kernels, body(): pl.pallas_call(functools.partial(step_kernel, n_rep, n_tp), out_shape=(ja...  34.1 us
    pallas_call x1, Pallas kernels, body(): pl.pallas_call(place_kernel, out_shape=(jax.ShapeDtypeStruct(rows.shape,...  7.01 us

profile of v2, /device:TPU:0, one launch (start us, length us, event | category | flops | bytes accessed | tf_op | source)
XLA Modules:
  0.0 41.7 jit_solution(15422430735805419228)
XLA Ops:
  0.6 34.1 %step.1 = (bf16[16,1024]{1,0:T(8,128)(2,1)}, f32[16,4,64,128]{3,2,1,0:T(8,128)}, f32[2,4,64,128]{3,2,1,0:T(8,128)}, bf16[2,4,128,256]{3,2,1,0:T(8,128)(2,1)}) custom-call(s32[16]{0:T(128)} %lengths_hbm.1, s32[16]{0:T(128)} %group_hbm.1, s32[16]{0:T(128)} %span_hbm.1, s32[1,2]{1,0:T(1,128)} %out_slot_hbm.3, s32[1,2]{1,0:T(1,128)} %move_dest_hbm.1, ...), custom_call_target="tpu_custom_call" | custom-call | tf_op jit(solution)/shard_map/step/pallas_call | solution.py:521
  34.7 7.0 %place.1 = (bf16[16,1024]{1,0:T(8,128)(2,1)}, bf16[16,4,128,256]{3,2,1,0:T(8,128)(2,1)}, f32[16,4,64,128]{3,2,1,0:T(8,128)}) custom-call(s32[2,16]{1,0:T(2,128)} %bitcast.12, s32[1,2]{1,0:T(1,128)} %out_slot_hbm.3, bf16[16,1024]{1,0:T(8,128)(2,1)} %get-tuple-element.10.rows_hbm, bf16[16,4,128,256]{3,2,1,0:T(8,128)(2,1)} %pool.1, ...), custom_call_target="tpu_custom_call" | custom-call | tf_op jit(solution)/shard_map/place/pallas_call | solution.py:560

commit v3 on v2

--- a/solution.py
+++ b/solution.py
@@ -50,7 +50,7 @@
     norm_attn, norm_mlp, tokens, qkvw, pool, prefix, mem, outw, gatew, upw, downw, mem_new,
     qbuf, dtab, part_send, part_recv, ar_one, ar_two, row_buf, held_page, held_mem,
     pick_page, pick_mem,
-    small_sem, load_sem, out_sem, q_send, q_recv, d_send, d_recv, part_sem, one_send, one_recv,
+    dests, dest_sem, small_sem, load_sem, out_sem, q_send, q_recv, d_send, d_recv, part_sem, one_send, one_recv,
     two_send, two_recv, row_send, row_recv, page_send, page_recv, mem_send, mem_recv,
 ):
     n_req, model_dim = tokens.shape
@@ -86,9 +86,9 @@
         (tokens_hbm, tokens), (qkvw_hbm, qkvw), (pool_hbm, pool), (prefix_hbm, prefix),
         (mem_hbm, mem), (outw_hbm, outw), (gatew_hbm, gatew), (upw_hbm, upw), (downw_hbm, downw),
     ]):
-        copy = pltpu.make_async_copy(src, dst, load_sem.at[i])
-        copy.start()
-        loads.append(copy)
+        loads.append(pltpu.make_async_copy(src, dst, load_sem.at[i]))
+    for copy in loads[:2]:
+        copy.start()
 
     barrier = pltpu.get_barrier_semaphore()
     for o in range(1, n_tp):
@@ -136,6 +136,8 @@
         tags = jnp.where(lane == m, move_dest[0, m], tags)
     dtab[rep] = tags
     loads[1].wait()
+    for copy in loads[2:5]:
+        copy.start()
     qkv = jnp.dot(normed, qkvw[...], preferred_element_type=f32).astype(bf16)
     for b in range(own_blocks):
         qbuf[tp * own_blocks + b] = qkv[:, b * block:(b + 1) * block]
@@ -175,7 +177,7 @@
                                rep_flip(1)))
 
     def dest_of(r, m):
-        return dtab[r][0:1, m:m + 1]
+        return dests[r, 0, m]
 
     def slot_rep(k, j):
         there = rep if j < 2 else rep_flip(first_bits[k])
@@ -227,6 +229,8 @@
                     out_ref[m, s, pl.ds(k * rows, rows)] = out.astype(out_ref.dtype)
 
     loads[2].wait()
+    for copy in loads[5:]:
+        copy.start()
     for m in range(n_move):
         page = table[half, out_slot[0, m]]
         for s in range(n_sect):
@@ -244,11 +248,15 @@
     group_col = column(lambda r: group[r], n_req)
     span_col = column(lambda r: span[r], n_req)
     keys_at = lax.broadcasted_iota(i32, (n_req, n_pool * page_len), 1)
-    live_pool = (keys_at // page_len == page_col) & (
-        keys_at % page_len + half * page_len < length_col
-    )
+    page_from = page_col * page_len
+    live_count = jnp.minimum(length_col - half * page_len, page_len)
+    live_pool = (keys_at >= page_from) & (keys_at < page_from + live_count)
     pre_at = lax.broadcasted_iota(i32, (n_req, n_group * pre_len), 1)
-    live_pre = pre_at // pre_len == group_col
+    live_pre = (pre_at >= group_col * pre_len) & (pre_at < (group_col + 1) * pre_len)
+    mem_at = lax.broadcasted_iota(i32, (n_req, n_req * half_dim), 1)
+    mem_from = lax.broadcasted_iota(i32, (n_req, n_req * half_dim), 0) * half_dim
+    mine = (mem_at >= mem_from) & (mem_at < mem_from + half_dim)
+    writes = mine & (span_col == 1)
     loads[3].wait()
     wait_all(q_copies)
 
@@ -262,7 +270,11 @@
     new_values = [head_rows(2, s).astype(f32) for s in range(n_sect)]
     wide = lax.broadcasted_iota(i32, (n_req, 128), 1)
     stats = jnp.zeros((n_req, 128), f32)
-    tops, denoms, accs = [], [], []
+    tops, denoms, accs, others = [], [], [], []
+
+    def own_half(x):
+        return jnp.where(half == 0, x[:, :half_dim], x[:, half_dim:])
+
     for s in range(n_sect):
         q = queries[s]
         k_pool = pool[:, s, :, :head_dim].reshape(n_pool * page_len, head_dim)
@@ -286,13 +298,18 @@
             jnp.concatenate(split2(w_pre), axis=0), v_pre, preferred_element_type=f32
         )
         acc = both[:n_req] + both[n_req:] + w_own * new_values[s]
-        part_send[s] = acc
         stats = jnp.where(wide == s, top, stats)
         stats = jnp.where(wide == 64 + s, denom, stats)
         tops.append(top)
         denoms.append(denom)
-        accs.append(acc)
-    part_send[n_sect] = stats
+        accs.append(own_half(acc))
+        others.append(jnp.where(half == 0, acc[:, half_dim:], acc[:, :half_dim]))
+    if n_sect % 2:
+        others.append(jnp.zeros((n_req, half_dim), f32))
+    n_pair = len(others) // 2
+    for s in range(n_pair):
+        part_send[s] = jnp.concatenate(others[2 * s:2 * s + 2], axis=1)
+    part_send[n_pair] = stats
     partner = lax.rem(tp + n_tp // 2, n_tp)
     part_copy = pltpu.make_async_remote_copy(
         src_ref=part_send, dst_ref=part_recv, send_sem=part_sem.at[0], recv_sem=part_sem.at[1],
@@ -301,14 +318,7 @@
     part_copy.start()
 
     loads[4].wait()
-    mem_at = lax.broadcasted_iota(i32, (n_req, n_req * half_dim), 1)
-    mem_row = lax.broadcasted_iota(i32, (n_req, n_req * half_dim), 0)
-    mine = mem_at // half_dim == mem_row
-    writes = mine & (span_col == 1)
     recalls, predicts, units = [], [], []
-
-    def own_half(x):
-        return jnp.where(half == 0, x[:, :half_dim], x[:, half_dim:])
 
     for s in range(n_sect):
         q_hi, q_lo = split2(unit_rows(queries[s].astype(f32)))
@@ -325,23 +335,27 @@
         predicts.append(seen[n_req:])
         units.append((k_hi, k_lo))
     wait_all(d_copies)
+    dest_copy = pltpu.make_async_copy(dtab, dests, dest_sem)
+    dest_copy.start()
     route_forward(page_copies, held_page, page_send, page_recv)
 
     part_copy.wait()
-    theirs = part_recv[n_sect]
+    theirs = part_recv[n_pair]
     mixed = []
     for s in range(n_sect):
         top_b = jnp.sum(jnp.where(wide == s, theirs, 0.0), axis=-1, keepdims=True)
         den_b = jnp.sum(jnp.where(wide == 64 + s, theirs, 0.0), axis=-1, keepdims=True)
         top = jnp.maximum(tops[s], top_b)
         w_a, w_b = jnp.exp(tops[s] - top), jnp.exp(top_b - top)
-        total = accs[s] * w_a + part_recv[s] * w_b
+        came = part_recv[s // 2][:, (s % 2) * half_dim:(s % 2 + 1) * half_dim]
+        total = accs[s] * w_a + came * w_b
         attended = total / (denoms[s] * w_a + den_b * w_b)
-        mixed.append(own_half(attended) + recalls[s])
+        mixed.append(attended + recalls[s])
     mixed = mixed[0] if n_sect == 1 else jnp.concatenate(mixed, axis=1)
     loads[5].wait()
     ar_one[tp] = jnp.dot(mixed.astype(bf16), outw[...], preferred_element_type=f32).astype(bf16)
     one_copies = tp_gather(ar_one.at[tp], one_send, one_recv)
+    dest_copy.wait()
     route_last(page_copies, held_page, pick_page, page_send, page_recv)
 
     for s in range(n_sect):
@@ -450,37 +464,42 @@
     n_head = rows_hbm.shape[1] // mem.shape[3]
     n_move = out_slot.shape[1]
     half = (lax.axis_index("tp") * n_sect) // n_head
+    page_loads, mem_loads = [], []
+    for m in range(n_move):
+        page_loads.append(pltpu.make_async_copy(
+            pages_in.at[m], page_buf.at[n_pool + m], page_load.at[n_pool + m]))
+        mem_loads.append(pltpu.make_async_copy(
+            mem_in.at[m], mem_buf.at[n_req + m], mem_load.at[n_req + m]))
+    for p in range(n_pool):
+        page_loads.append(pltpu.make_async_copy(pool.at[p], page_buf.at[p], page_load.at[p]))
+    for r in range(n_req):
+        mem_loads.append(pltpu.make_async_copy(mem.at[r], mem_buf.at[r], mem_load.at[r]))
+    for copy in page_loads + mem_loads:
+        copy.start()
     for copy in smalls[:2]:
         copy.wait()
     slots = [out_slot[0, m] for m in range(n_move)]
     pages = [table[half, slot] for slot in slots]
-
-    def fetch(index, moved, kept, arrived, buf, sem):
-        stays = index >= 0
+    outs = []
+
+    def store(index, count, moved, buf, out, sem):
+        source = jnp.int32(index)
         for m in range(n_move):
-            stays = stays & (index != moved[m])
-
-            @pl.when(index == moved[m])
-            def _(m=m):
-                pltpu.make_async_copy(arrived.at[m], buf.at[index], sem).start()
-
-        @pl.when(stays)
-        def _():
-            pltpu.make_async_copy(kept.at[index], buf.at[index], sem).start()
-
+            source = jnp.where(moved[m] == index, count + m, source)
+        copy = pltpu.make_async_copy(buf.at[source], out.at[index], sem.at[index])
+        copy.start()
+        outs.append(copy)
+
+    for copy in page_loads[:n_move]:
+        copy.wait()
     for p in range(n_pool):
-        fetch(jnp.int32(p), pages, pool, pages_in, page_buf, page_load.at[p])
+        page_loads[n_move + p].wait()
+        store(p, n_pool, pages, page_buf, pool_out, page_sem)
+    for copy in mem_loads[:n_move]:
+        copy.wait()
     for r in range(n_req):
-        fetch(jnp.int32(r), slots, mem, mem_in, mem_buf, mem_load.at[r])
-    outs = []
-    for p in range(n_pool):
-        pltpu.make_async_copy(pool.at[p], page_buf.at[p], page_load.at[p]).wait()
-        outs.append(pltpu.make_async_copy(page_buf.at[p], pool_out.at[p], page_sem.at[p]))
-        outs[-1].start()
-    for r in range(n_req):
-        pltpu.make_async_copy(mem.at[r], mem_buf.at[r], mem_load.at[r]).wait()
-        outs.append(pltpu.make_async_copy(mem_buf.at[r], mem_out.at[r], mem_sem.at[r]))
-        outs[-1].start()
+        mem_loads[n_move + r].wait()
+        store(r, n_req, slots, mem_buf, mem_out, mem_sem)
     smalls[2].wait()
     for copy in outs:
         copy.wait()
@@ -533,8 +552,8 @@
         ] + [
             V((n_tp * columns // block, n_req, block), bf16),
             V((n_rep, 8, 128), i32),
-            V((n_sect + 1, n_req, 128), f32),
-            V((n_sect + 1, n_req, 128), f32),
+            V(((n_sect + 1) // 2 + 1, n_req, 128), f32),
+            V(((n_sect + 1) // 2 + 1, n_req, 128), f32),
             V((n_tp, n_req, model_dim), bf16),
             V((n_tp, n_req, model_dim), bf16),
             V((n_rep, row_len, 128), bf16),
@@ -542,6 +561,7 @@
             V(lead + mem_piece, bf16),
             V(page_pick, bf16),
             V(mem_pick, bf16),
+            pltpu.SMEM((n_rep, 8, 128), i32), dma,
             dma((10,)), dma((9,)), dma,
             dma((n_tp - 1,)), dma((n_tp - 1,)),
             dma((n_rep - 1,)), dma((n_rep - 1,)),
@@ -568,8 +588,10 @@
         out_specs=(vmem, hbm, hbm),
         scratch_shapes=[
             pltpu.SMEM(table.shape, i32), pltpu.SMEM(out_slot.shape, i32),
-            V(cache_pool.shape, bf16), V(memory.shape, f32),
-            dma((3,)), dma((n_pool,)), dma((n_req,)), dma((n_pool,)), dma((n_req,)),
+            V((n_pool + n_move,) + cache_pool.shape[1:], bf16),
+            V((n_req + n_move,) + memory.shape[1:], f32),
+            dma((3,)), dma((n_pool + n_move,)), dma((n_req + n_move,)), dma((n_pool,)),
+            dma((n_req,)),
         ],
         compiler_params=pltpu.CompilerParams(vmem_limit_bytes=VMEM_BYTES),
         name="place",

time: 41.9 us -> 38.6 us (0.921)
  Pallas kernels: 41.1 us -> 37.8 us
    pallas_call x1, Pallas kernels: 34.1 us -> 31.3 us  [body(): pl.pallas_call(functools.partial(step_kernel, n_rep, n_tp), out_shape=(ja...]
    pallas_call x1, Pallas kernels: 7.01 us -> 6.5 us  [body(): pl.pallas_call(place_kernel, out_shape=(jax.ShapeDtypeStruct(rows.shape,...]
where the time goes in v3:
time: 38.6 us; the launch traced here: 38.4 us
  Pallas kernels  37.8 us (98%)
  between operations  0.65 us (2%)
    pallas_call x1, Pallas kernels, body(): pl.pallas_call(functools.partial(step_kernel, n_rep, n_tp), out_shape=(ja...  31.3 us
    pallas_call x1, Pallas kernels, body(): pl.pallas_call(place_kernel, out_shape=(jax.ShapeDtypeStruct(rows.shape,...  6.5 us

profile of v3, /device:TPU:0, one launch (start us, length us, event | category | flops | bytes accessed | tf_op | source)
XLA Modules:
  0.0 38.4 jit_solution(373977210043234722)
XLA Ops:
  0.6 31.3 %step.1 = (bf16[16,1024]{1,0:T(8,128)(2,1)}, f32[16,4,64,128]{3,2,1,0:T(8,128)}, f32[2,4,64,128]{3,2,1,0:T(8,128)}, bf16[2,4,128,256]{3,2,1,0:T(8,128)(2,1)}) custom-call(s32[16]{0:T(128)} %lengths_hbm.1, s32[16]{0:T(128)} %group_hbm.1, s32[16]{0:T(128)} %span_hbm.1, s32[1,2]{1,0:T(1,128)} %out_slot_hbm.3, s32[1,2]{1,0:T(1,128)} %move_dest_hbm.1, ...), custom_call_target="tpu_custom_call" | custom-call | tf_op jit(solution)/shard_map/step/pallas_call | solution.py:540
  31.9 6.5 %place.1 = (bf16[16,1024]{1,0:T(8,128)(2,1)}, bf16[16,4,128,256]{3,2,1,0:T(8,128)(2,1)}, f32[16,4,64,128]{3,2,1,0:T(8,128)}) custom-call(s32[2,16]{1,0:T(2,128)} %bitcast.12, s32[1,2]{1,0:T(1,128)} %out_slot_hbm.3, bf16[16,1024]{1,0:T(8,128)(2,1)} %get-tuple-element.10.rows_hbm, bf16[16,4,128,256]{3,2,1,0:T(8,128)(2,1)} %pool.1, ...), custom_call_target="tpu_custom_call" | custom-call | tf_op jit(solution)/shard_map/place/pallas_call | solution.py:580
